TPU v7x, 512 devices: a whole 4x4x16 slice. The times are simulated.
512 devices in a mesh: tm: 8 (over x, y_hi), array: 64 (over z, y_lo, core).
Axes of the slice: x: 4, y: 4 (y_hi: 2, y_lo: 2; y = y_hi * 2 + y_lo), z: 16, core: 2. Of those that a mesh axis runs over, the one named last changes fastest.
Arguments:
- raw_strain: bfloat16 [8, 8192, 1024], P('tm', 'array'), may hold values from -6 to 6
- fir_taps: float32 [8], replicated, may hold values from -3 to 3
- source_ids: int32 [4, 32], replicated, may hold values from 0 to 8191, as said below
Outputs:
- stacked: bfloat16 [128, 101, 8192], P('tm', None, 'array')
Inputs may be any that keep to these rules, and one draw needn't show every extreme that they name: `source_ids`: channel ids of the virtual sources.
All inputs are finite; a program needn't handle non-finite values.
Results may differ from a plain program's by a relative error of at most 0.017.
Values may be sent and summed in bfloat16 or wider, within the bound.
A program may use at most 128 MiB of HBM per device.

v0:
```python
import math

import jax
import jax.numpy as jnp
from jax import lax
from jax.sharding import PartitionSpec as P

SOURCES = 128
MAXLAG = 50
WINDOW = 64
DECIM = 4
NTAP = 8
SAMPLES = 256
LAGS = 101


epsilon = 1e-05
lag_group = 17


def decimate(raw_segment, fir_taps):
    phases = [raw_segment[:, phase_index::DECIM] for phase_index in range(DECIM)]
    filtered = jnp.zeros((raw_segment.shape[0], SAMPLES), jnp.float32)
    for tap_index in range(NTAP):
        phase_index = -tap_index % DECIM
        delay = (tap_index + phase_index) // DECIM
        shifted = jnp.pad(phases[phase_index], ((0, 0), (delay, 0)))[:, :SAMPLES]
        filtered = filtered + fir_taps[tap_index] * shifted.astype(jnp.float32)
    return filtered


def normalize(filtered):
    half_window = WINDOW // 2
    window_sum = jnp.pad(jnp.abs(filtered), ((0, 0), (half_window, 0)))
    span_now = 1
    while span_now < WINDOW:
        window_sum = window_sum + jnp.pad(window_sum[:, span_now:], ((0, 0), (0, span_now)))
        span_now = span_now * 2
    window_sum = window_sum[:, :SAMPLES]
    return (filtered / (window_sum * (1.0 / WINDOW) + epsilon)).astype(jnp.bfloat16)


def correlate(source_rows, normed):
    row_total = source_rows.shape[0]
    block_size = min(32, row_total)
    padded = jnp.pad(source_rows, ((0, 0), (MAXLAG, MAXLAG)))
    results = []
    for first_row in range(0, row_total, block_size):
        block_rows = padded[first_row : first_row + block_size]
        lag_parts = []
        for first_lag in range(0, LAGS, lag_group):
            lag_range = range(first_lag, min(first_lag + lag_group, LAGS))
            lagged = jnp.stack(
                [
                    block_rows[:, 2 * MAXLAG - lag_index : 2 * MAXLAG - lag_index + SAMPLES]
                    for lag_index in lag_range
                ],
                1,
            )
            lag_parts.append(
                lax.dot_general(
                    lagged, normed, (((2,), (1,)), ((), ())), preferred_element_type=jnp.float32
                )
            )
        results.append(jnp.concatenate(lag_parts, 1))
    return jnp.concatenate(results, 0)


def body(raw_strain, fir_taps, source_ids):
    normed = normalize(decimate(raw_strain[0], fir_taps))
    width_dev = normed.shape[0]
    local_ids = source_ids - lax.axis_index("array") * width_dev
    selector = (local_ids[:, :, None] == jnp.arange(width_dev, dtype=jnp.int32)).astype(
        jnp.bfloat16
    )
    picked = jnp.dot(
        selector.reshape(SOURCES, width_dev), normed, preferred_element_type=jnp.float32
    )
    source_rows = lax.psum(picked, "array").astype(jnp.bfloat16)
    factor = 1.0 / math.sqrt(SAMPLES)
    groups = lax.axis_size("tm")
    partial_value = correlate(source_rows, normed) * factor
    stacked_sum = lax.psum_scatter(
        partial_value.astype(jnp.bfloat16), "tm", scatter_dimension=0, tiled=True
    ).astype(jnp.float32)
    return (stacked_sum * (1.0 / math.sqrt(groups))).astype(jnp.bfloat16)


def solution(mesh):
    return jax.shard_map(
        body,
        mesh=mesh,
        in_specs=(P("tm", "array", None), P(), P()),
        out_specs=P("tm", None, "array"),
        check_vma=False,
    )
```

profile of v0, /device:TPU:1, one launch (start us, length us, event | category | flops | bytes accessed | tf_op | source)
XLA Modules:
  0.0 377.0 jit_solution(12649795659059110846)
XLA Ops:
  6.5 3.2 slice.1711
  9.8 3.2 slice.1708
  13.0 3.2 slice.1705
  16.3 3.2 slice.1703
  19.5 0.7 broadcast_subtract_fusion
  20.3 1.6 fusion.434
  21.9 5.3 %fusion.433 = (f32[128,256]{1,0:T(8,128)S(1)}, f32[128,256]{1,0:T(8,128)S(1)}) fusion(bf16[128,256]{1,0:T(8,128)(2,1)S(1)} %slice.1711, f32[]{:T(128)} %bitcast.8, bf16[128,256]{1,0:T(8,128)(2,1)S(1)} %slice.1708, f32[]{:T(128)} %bitcast.7, bf16[128,256]{1,0:T(8,128)(2,1)S(1)} %slice.1705, f32[]{:T(128)} %bitcast.6, bf16[128,256]{1,0:T(8,128)(2,1)S(1)} %slice.1703, ...), kind=kLoop, calls=%fused_computation.1284 | loop fusion | flops 786432 | bytes 524320 | tf_op jit(solution)/shard_map/abs | solution.py:34
  27.3 0.1 pad_slice_fusion.401
  27.4 0.2 fusion.2
  27.6 0.1 fusion.1
  27.7 0.1 slice.2134
  27.8 0.1 slice.2135
  28.0 0.1 slice.2136
  28.3 0.2 fusion.31
  28.5 214.6 %all-reduce.16 = bf16[128,256]{1,0:T(8,128)(2,1)S(1)} all-reduce(f32[128,256]{1,0:T(8,128)S(1)} %fusion.31), channel_id=1, replica_groups=mesh['tm'=8,'array'=64] {'array'}, use_global_device_ids=true, to_apply=%region_0.1 | all-reduce | flops 32768 | bytes 196608 | tf_op jit(solution)/shard_map/psum | solution.py:79
  245.7 0.1 constant_dynamic-update-slice_fusion.85
  247.0 0.1 constant_dynamic-update-slice_fusion.68
  252.4 0.1 constant_dynamic-update-slice_fusion.186
  259.1 0.1 constant_dynamic-update-slice_fusion.34
  259.2 0.1 constant_dynamic-update-slice_fusion.15
  261.4 0.1 constant_dynamic-update-slice_fusion.287
  266.7 0.2 convolution_dynamic-update-slice_fusion.4
  267.0 0.2 convolution_dynamic-update-slice_fusion.19
  267.3 0.2 convolution_dynamic-update-slice_fusion.9
  267.5 0.2 convolution_dynamic-update-slice_fusion.14
  267.7 0.2 convolution_dynamic-update-slice_fusion.3
  268.0 0.2 convolution_dynamic-update-slice_fusion.2
  268.2 0.2 convolution_dynamic-update-slice_fusion.1
  268.4 0.2 convolution_dynamic-update-slice_fusion
  268.7 0.2 convolution_dynamic-update-slice_fusion.20
  268.9 0.2 convolution_dynamic-update-slice_fusion.18
  269.1 0.2 convolution_dynamic-update-slice_fusion.17
  269.3 0.2 convolution_dynamic-update-slice_fusion.16
  269.6 0.2 convolution_dynamic-update-slice_fusion.15
  269.8 0.2 convolution_dynamic-update-slice_fusion.23
  270.1 0.2 convolution_dynamic-update-slice_fusion.8
  270.3 0.2 convolution_dynamic-update-slice_fusion.7
  270.5 0.2 convolution_dynamic-update-slice_fusion.6
  270.8 0.2 convolution_dynamic-update-slice_fusion.5
  271.0 0.2 convolution_dynamic-update-slice_fusion.21
  271.2 0.2 convolution_dynamic-update-slice_fusion.13
  271.5 0.2 convolution_dynamic-update-slice_fusion.12
  271.7 0.2 convolution_dynamic-update-slice_fusion.11
  271.9 0.2 convolution_dynamic-update-slice_fusion.10
  272.2 0.2 convolution_dynamic-update-slice_fusion.22
  272.4 2.1 fusion
  274.5 93.8 %reduce-scatter.2.cloned.1.call-done = bf16[16,101,128]{2,0,1:T(8,128)(2,1)} async-done(((bf16[128,101,128]{2,0,1:T(8,128)(2,1)}), bf16[16,101,128]{2,0,1:T(8,128)(2,1)}) %reduce-scatter.2.cloned.1.call-update) | async-done | bytes 413712 | tf_op jit(solution)/shard_map/reduce_scatter | solution.py:83
  368.3 1.8 multiply_convert_fusion
  (301 shorter events, 23.1 us)
Async XLA Ops:
  6.5 361.8 %reduce-scatter.2.cloned.1.call-start = ((), (), s32[]{:S(2)}) async-start(), calls=%async_computation.1 | async-start | bytes 3723264 | tf_op jit(solution)/shard_map/reduce_scatter | solution.py:83
Sparse Core Ops, SparseCore 0:
  274.7 93.6 reduce-scatter.1
where the time goes:
time: 378 us; the launch traced here: 377 us
  blocking collectives  215 us (57%)
  waiting for transfers between devices  93.8 us (25%)
  local copies, waits for them, and re-layouts  38.7 us (10%)
  between operations  14 us (4%)
  other arithmetic  10.4 us (3%)
  matrix products  5.61 us (1%)
    psum x1, blocking collectives, body(): source_rows = lax.psum(picked, 'array').astype(jnp.bfloat16)  215 us
    reduce_scatter x1, waiting for transfers between devices, body(): lax.psum_scatter(partial_value.astype(jnp.bfloat16), 'tm', scatter_dimens...  93.8 us
    unnamed x279, local copies, waits for them, and re-layouts  21.6 us
    slice x4, local copies, waits for them, and re-layouts, decimate(): raw_segment[:, phase_index::DECIM]  12.9 us
  transfers between devices with their start and end apart: 1, of which 1 were waited for; matrix products, arithmetic and copies ran while one was open for 0% of the time, Pallas kernels for 0%

commit v1 on v0

v1 whole, which is shorter than its diff:
```python
import functools
import math

import jax
import jax.numpy as jnp
from jax import lax
from jax.experimental import pallas as pl
from jax.experimental.pallas import tpu as pltpu
from jax.sharding import PartitionSpec as P

MESH = pl.DeviceIdType.MESH
SOURCES = 128
MAXLAG = 50
WINDOW = 64
DECIM = 4
NTAP = 8
SAMPLES = 256
LAGS = 101
RAW = 1024
SEG = 8
ROWS = 16
CH = 128
NZ = 16
NYC = 4
LPAD = 104
UP = 26
DOWN = 25
EPSILON = 1e-05
SCALE = 1.0 / (math.sqrt(SAMPLES) * math.sqrt(SEG))

f32 = jnp.float32
bf16 = jnp.bfloat16
NT = (((1,), (1,)), ((), ()))
TN = (((0,), (0,)), ((), ()))


def iota(shape, dim):
    return lax.broadcasted_iota(jnp.int32, shape, dim)


def terms(value, count):
    parts = []
    for _ in range(count):
        part = value.astype(bf16)
        parts.append(part)
        value = value - part.astype(f32)
    return parts


def normalize(raw, taps_ref):
    k = DECIM * iota((128, 128), 1) - iota((128, 128), 0)
    band = jnp.zeros((128, 128), f32)
    for tap in range(NTAP):
        band = jnp.where(k == tap, taps_ref[tap], band)
    band = jnp.concatenate([band, jnp.zeros((128, 128), f32)], 1)
    lane = iota((128, SAMPLES), 1)
    filtered = jnp.zeros((CH, SAMPLES), f32)
    for tile in range(RAW // 128):
        placed = pltpu.roll(band, 32 * tile, 1) if tile else band
        if tile == RAW // 128 - 1:
            placed = jnp.where(lane < 2, 0.0, placed)
        piece = raw[:, 128 * tile : 128 * (tile + 1)]
        for part in terms(placed, 3):
            filtered = filtered + jnp.dot(piece, part, preferred_element_type=f32)
    gap = iota((SAMPLES, SAMPLES), 0) - iota((SAMPLES, SAMPLES), 1)
    window = jnp.where((gap >= -(WINDOW // 2)) & (gap < WINDOW // 2), 1.0, 0.0).astype(bf16)
    total = jnp.zeros((CH, SAMPLES), f32)
    for part in terms(jnp.abs(filtered), 2):
        total = total + jnp.dot(part, window, preferred_element_type=f32)
    return filtered / (total * (1.0 / WINDOW) + EPSILON)


def kernel(
    raw_ref, taps_ref, ids_ref, out_ref,
    xall, send1, recv1, mine2, recv2, mine3, rows, lhs_up, lhs_down, corr,
    x_send, x_recv, s1_send, s1_recv, s2_send, s2_recv, s3_send, s3_recv,
):
    tm = lax.axis_index("tm")
    place = lax.axis_index("array")
    z = lax.div(place, NYC)
    yc = lax.rem(place, NYC)
    owner = lax.div(z, 2)
    half = lax.rem(z, 2)
    own = tm == owner

    def along_z(d):
        return {"tm": tm, "array": lax.rem(z + d, NZ) * NYC + yc}

    def along_yc(d):
        return {"tm": tm, "array": z * NYC + lax.rem(yc + d, NYC)}

    def along_tm(d):
        return {"tm": lax.rem(tm + d, SEG), "array": place}

    def to_owner(d):
        return {"tm": owner, "array": lax.rem(z + d, NZ) * NYC + yc}

    barrier = pltpu.get_barrier_semaphore()

    def greet(device):
        pl.semaphore_signal(barrier, inc=1, device_id=device, device_id_type=MESH)

    for d in range(1, NZ):
        greet(along_z(d))
    for d in range(1, NYC):
        greet(along_yc(d))
    for d in range(1, SEG):
        greet(along_tm(d))
    for g in range(SEG):
        for h in range(2):
            sender = {"tm": g, "array": (2 * tm + h) * NYC + yc}
            pl.when(jnp.logical_not((tm == g) & (z == 2 * tm + h)))(functools.partial(greet, sender))

    normed = normalize(raw_ref[0], taps_ref)
    xall[tm] = normed.astype(bf16)

    ids = jnp.concatenate([ids_ref[r : r + 1, :] for r in range(4)], 1)
    chosen = (iota((CH, SOURCES), 0) == ids - place * CH).astype(f32).astype(bf16)
    picked = lax.dot_general(chosen, xall[tm], TN, preferred_element_type=f32)
    for chunk in range(NZ):
        part = picked[8 * chunk : 8 * chunk + 8]
        send1[chunk] = jnp.concatenate([part[:, :128], part[:, 128:]], 0).astype(bf16)

    @pl.when(own)
    def _():
        pl.semaphore_wait(barrier, NZ - 1 + NYC - 1 + SEG - 1 + 15)

    @pl.when(jnp.logical_not(own))
    def _():
        pl.semaphore_wait(barrier, NZ - 1 + NYC - 1 + SEG - 1 + 16)

    first = [
        pltpu.make_async_remote_copy(
            send1.at[lax.rem(z + d, NZ)], recv1.at[d], s1_send.at[d], s1_recv.at[d], along_z(d), MESH
        )
        for d in range(1, NZ)
    ]
    for copy in first:
        copy.start()
    gather = [
        pltpu.make_async_remote_copy(
            xall.at[tm], xall.at[tm], x_send.at[d], x_recv.at[d], along_tm(d), MESH
        )
        for d in range(1, SEG)
    ]
    for copy in gather:
        copy.start()

    total = send1[z].astype(f32)
    for d in range(1, NZ):
        first[d - 1].wait_recv()
        total = total + recv1[d].astype(f32)
    mine2[...] = total.astype(bf16)
    second = [
        pltpu.make_async_remote_copy(
            mine2, recv2.at[d], s2_send.at[d], s2_recv.at[d], along_yc(d), MESH
        )
        for d in range(1, NYC)
    ]
    for copy in second:
        copy.start()
    for d in range(1, NYC):
        second[d - 1].wait_recv()
        total = total + recv2[d].astype(f32)
    mine3[...] = total.astype(bf16)

    slot = 2 * tm + half
    third = [
        pltpu.make_async_remote_copy(
            mine3, rows.at[slot], s3_send.at[d], s3_recv.at[slot], to_owner(d), MESH
        )
        for d in range(NZ)
    ]
    for copy in third[1:]:
        copy.start()
    here = pltpu.make_async_copy(mine3, rows.at[slot], s3_recv.at[slot])
    pl.when(own)(lambda: here.start())
    pl.when(jnp.logical_not(own))(lambda: third[0].start())

    for g in range(SEG):
        for h in range(2):
            pltpu.make_async_copy(rows.at[2 * g + h], rows.at[2 * g + h], s3_recv.at[2 * g + h]).wait()

    lane = iota((ROWS, 128), 1)
    for g in range(SEG):
        a = rows[2 * g].astype(f32)
        b = rows[2 * g + 1].astype(f32)
        low = jnp.concatenate([a[:8], b[:8]], 0)
        high = jnp.concatenate([a[8:], b[8:]], 0)
        for i in range(UP):
            q = 2 * i
            lo, hi = (pltpu.roll(low, q, 1), pltpu.roll(high, q, 1)) if q else (low, high)
            lhs_up[ROWS * i : ROWS * (i + 1), 256 * g : 256 * g + 128] = jnp.where(lane < q, 0.0, lo).astype(bf16)
            lhs_up[ROWS * i : ROWS * (i + 1), 256 * g + 128 : 256 * g + 256] = jnp.where(lane < q, lo, hi).astype(bf16)
        for i in range(DOWN):
            q = 128 - (2 * i + 1)
            lo, hi = pltpu.roll(low, q, 1), pltpu.roll(high, q, 1)
            lhs_down[ROWS * i : ROWS * (i + 1), 256 * g : 256 * g + 128] = jnp.where(lane < q, lo, hi).astype(bf16)
            lhs_down[ROWS * i : ROWS * (i + 1), 256 * g + 128 : 256 * g + 256] = jnp.where(lane < q, hi, 0.0).astype(bf16)

    for copy in gather:
        copy.wait_recv()

    wide = iota((CH, SAMPLES), 1)
    up = jnp.zeros((ROWS * UP, 256), f32)
    down = jnp.zeros((ROWS * DOWN, 256), f32)
    for g in range(SEG):
        x = xall[g]
        later = pltpu.roll(x.astype(f32), SAMPLES - 1, 1)
        later = jnp.where(wide == SAMPLES - 1, 0.0, later).astype(bf16)
        earlier = pltpu.roll(x.astype(f32), 1, 1)
        earlier = jnp.where(wide == 0, 0.0, earlier).astype(bf16)
        cols = slice(256 * g, 256 * g + 256)
        up = up + lax.dot_general(
            lhs_up[:, cols], jnp.concatenate([x, later], 0), NT, preferred_element_type=f32
        )
        down = down + lax.dot_general(
            lhs_down[:, cols], jnp.concatenate([x, earlier], 0), NT, preferred_element_type=f32
        )

    for i in range(UP):
        block = up[ROWS * i : ROWS * (i + 1)] * SCALE
        lag = MAXLAG + 2 * i
        corr[pl.ds(lag, ROWS, stride=LPAD), :] = block[:, :128]
        if lag + 1 < LAGS:
            corr[pl.ds(lag + 1, ROWS, stride=LPAD), :] = block[:, 128:]
    for i in range(DOWN):
        block = down[ROWS * i : ROWS * (i + 1)] * SCALE
        lag = MAXLAG - 1 - 2 * i
        corr[pl.ds(lag, ROWS, stride=LPAD), :] = block[:, :128]
        corr[pl.ds(lag - 1, ROWS, stride=LPAD), :] = block[:, 128:]
    for j in range(ROWS):
        out_ref[j] = corr[LPAD * j : LPAD * j + LAGS, :].astype(bf16)

    for copy in first + gather + second + third[1:]:
        copy.wait_send()
    pl.when(jnp.logical_not(own))(lambda: third[0].wait_send())


def body(raw_strain, fir_taps, source_ids):
    vmem = pl.BlockSpec(memory_space=pltpu.VMEM)
    dma = pltpu.SemaphoreType.DMA
    return pl.pallas_call(
        kernel,
        out_shape=jax.ShapeDtypeStruct((ROWS, LAGS, CH), bf16),
        in_specs=[vmem, pl.BlockSpec(memory_space=pltpu.SMEM), vmem],
        out_specs=vmem,
        scratch_shapes=[
            pltpu.VMEM((SEG, CH, SAMPLES), bf16),
            pltpu.VMEM((NZ, 16, 128), bf16),
            pltpu.VMEM((NZ, 16, 128), bf16),
            pltpu.VMEM((16, 128), bf16),
            pltpu.VMEM((NYC, 16, 128), bf16),
            pltpu.VMEM((16, 128), bf16),
            pltpu.VMEM((2 * SEG, 16, 128), bf16),
            pltpu.VMEM((ROWS * UP, SEG * SAMPLES), bf16),
            pltpu.VMEM((ROWS * DOWN, SEG * SAMPLES), bf16),
            pltpu.VMEM((ROWS * LPAD, CH), f32),
            dma((SEG,)), dma((SEG,)),
            dma((NZ,)), dma((NZ,)),
            dma((NYC,)), dma((NYC,)),
            dma((NZ,)), dma((2 * SEG,)),
        ],
        compiler_params=pltpu.CompilerParams(
            collective_id=0, has_side_effects=True, vmem_limit_bytes=40 * 1024 * 1024
        ),
    )(raw_strain, fir_taps, source_ids)


def solution(mesh):
    return jax.shard_map(
        body,
        mesh=mesh,
        in_specs=(P("tm", "array", None), P(), P()),
        out_specs=P("tm", None, "array"),
        check_vma=False,
    )
```

time: 378 us -> 45.8 us (0.12)
  the two profiles are of different devices: /device:TPU:1 before, /device:TPU:4 now
where the time goes in v1:
time: 45.8 us; the launch traced here: 45.6 us
  Pallas kernels  42.5 us (93%)
  local copies, waits for them, and re-layouts  3.09 us (7%)
    pallas_call x1, Pallas kernels, body(): pl.pallas_call(kernel, out_shape=jax.ShapeDtypeStruct((ROWS, LAGS, CH), b...  42.5 us
    unnamed x6, local copies, waits for them, and re-layouts  2.29 us

profile of v1, /device:TPU:4, one launch (start us, length us, event | category | flops | bytes accessed | tf_op | source)
XLA Modules:
  0.0 45.6 jit_solution(2975013793400459230)
XLA Ops:
  0.0 0.0 copy-start
  0.0 0.9 %copy-done = bf16[1,128,1024]{2,1,0:T(8,128)(2,1)S(1)} copy-done((bf16[1,128,1024]{2,1,0:T(8,128)(2,1)S(1)}, bf16[1,128,1024]{2,1,0:T(8,128)(2,1)}, u32[]{:S(2)}) %copy-start) | copy-done | bytes 262168
  1.0 0.0 copy-start.1
  1.0 0.7 %copy-done.1 = s32[4,32]{1,0:T(4,128)S(1)} copy-done((s32[4,32]{1,0:T(4,128)S(1)}, s32[4,32]{1,0:T(4,128)}, u32[]{:S(2)}) %copy-start.1) | copy-done | bytes 536
  1.6 0.0 copy-start.2
  1.6 0.7 %copy-done.2 = f32[8]{0:T(128)S(1)} copy-done((f32[8]{0:T(128)S(1)}, f32[8]{0:T(128)}, u32[]{:S(2)}) %copy-start.2) | copy-done | bytes 56
  2.3 42.5 %shard_map.37 = bf16[16,101,128]{2,1,0:T(8,128)(2,1)S(1)} custom-call(bf16[1,128,1024]{2,1,0:T(8,128)(2,1)S(1)} %copy-done, f32[8]{0:T(128)S(1)} %copy-done.2, s32[4,32]{1,0:T(4,128)S(1)} %copy-done.1), custom_call_target="tpu_custom_call" | custom-call | tf_op jit(solution)/shard_map/pallas_call | solution.py:243
  44.8 0.8 %copy.4 = bf16[16,101,128]{2,0,1:T(8,128)(2,1)} copy(bf16[16,101,128]{2,1,0:T(8,128)(2,1)S(1)} %shard_map.37) | data formatting | bytes 827392 | tf_op jit(solution)/shard_map/pallas_call | solution.py:243
Async XLA Ops:
  0.0 0.9 %copy-start = (bf16[1,128,1024]{2,1,0:T(8,128)(2,1)S(1)}, bf16[1,128,1024]{2,1,0:T(8,128)(2,1)}, u32[]{:S(2)}) copy-start(bf16[1,128,1024]{2,1,0:T(8,128)(2,1)} %raw_ref.1) | copy-start | bytes 786436
  1.0 0.7 %copy-start.1 = (s32[4,32]{1,0:T(4,128)S(1)}, s32[4,32]{1,0:T(4,128)}, u32[]{:S(2)}) copy-start(s32[4,32]{1,0:T(4,128)} %ids_ref.1) | copy-start | bytes 1540
  1.6 0.7 %copy-start.2 = (f32[8]{0:T(128)S(1)}, f32[8]{0:T(128)}, u32[]{:S(2)}) copy-start(f32[8]{0:T(128)} %taps_ref.1) | copy-start | bytes 100

commit v2 on v1

v2 whole, which is shorter than its diff:
```python
import functools
import math

import jax
import jax.numpy as jnp
from jax import lax
from jax.experimental import pallas as pl
from jax.experimental.pallas import tpu as pltpu
from jax.sharding import PartitionSpec as P

MESH = pl.DeviceIdType.MESH
SOURCES = 128
MAXLAG = 50
WINDOW = 64
DECIM = 4
NTAP = 8
SAMPLES = 256
LAGS = 101
RAW = 1024
SEG = 8
ROWS = 16
CH = 128
NZ = 16
NYC = 4
NEAR = 4
UP = 26
DOWN = 25
EPSILON = 1e-05
SCALE = 1.0 / (math.sqrt(SAMPLES) * math.sqrt(SEG))

f32 = jnp.float32
bf16 = jnp.bfloat16
TN = (((0,), (0,)), ((), ()))


def iota(shape, dim):
    return lax.broadcasted_iota(jnp.int32, shape, dim)


def terms(value, count):
    parts = []
    for _ in range(count):
        part = value.astype(bf16)
        parts.append(part)
        value = value - part.astype(f32)
    return parts


def tap_bands(taps_ref):
    k = DECIM * iota((128, 128), 1) - iota((128, 128), 0)
    band = jnp.zeros((128, 128), f32)
    for tap in range(NTAP):
        band = jnp.where(k == tap, taps_ref[tap], band)
    band = jnp.concatenate([band, jnp.zeros((128, 128), f32)], 1)
    lane = iota((128, SAMPLES), 1)
    bands = []
    for tile in range(RAW // 128):
        placed = pltpu.roll(band, 32 * tile, 1) if tile else band
        if tile == RAW // 128 - 1:
            placed = jnp.where(lane < 2, 0.0, placed)
        bands.append(terms(placed, 3))
    return bands


def normalize(raw, bands):
    filtered = jnp.zeros((CH, SAMPLES), f32)
    for term in range(3):
        matrix = jnp.concatenate([band[term] for band in bands], 0)
        filtered = filtered + jnp.dot(raw, matrix, preferred_element_type=f32)
    gap = iota((SAMPLES, SAMPLES), 0) - iota((SAMPLES, SAMPLES), 1)
    window = jnp.where((gap >= -(WINDOW // 2)) & (gap < WINDOW // 2), 1.0, 0.0).astype(bf16)
    total = jnp.zeros((CH, SAMPLES), f32)
    for part in terms(jnp.abs(filtered), 2):
        total = total + jnp.dot(part, window, preferred_element_type=f32)
    return filtered / (total * (1.0 / WINDOW) + EPSILON)


def kernel(
    raw_hbm, taps_hbm, ids_hbm, out_ref,
    raw, taps, ids_ref, xall, send1, recv1, mine2, recv2, mine3, parts, rows, lhs_up, lhs_down, rhs_up, rhs_down,
    in_sem, x_send, x_recv, s1_send, s1_recv, s2_send, s2_recv, s3_send, s3_recv, s4_send, s4_recv, column, ready,
):
    inputs = [
        pltpu.make_async_copy(src, dst, in_sem.at[i])
        for i, (src, dst) in enumerate(((taps_hbm, taps), (raw_hbm, raw), (ids_hbm, ids_ref)))
    ]
    for copy in inputs:
        copy.start()

    tm = lax.axis_index("tm")
    place = lax.axis_index("array")
    z = lax.div(place, NYC)
    yc = lax.rem(place, NYC)
    core = lax.rem(place, 2)
    owner = lax.rem(z, SEG)
    own = tm == owner

    def at(t, dz, side):
        return {"tm": t, "array": lax.rem(z + dz + NZ, NZ) * NYC + side}

    def along_z(d):
        return at(tm, d, yc)

    yc_peer = [None, yc + 1 - 2 * core, lax.rem(yc + 2, NYC), lax.rem(yc + 2, NYC) + 1 - 2 * core]

    def along_yc(d):
        return at(tm, 0, yc_peer[d])

    def along_tm(d):
        return at(lax.rem(tm + d, SEG), 0, yc)

    near = [-4, 4, -3, 3, -2, 2, -1, 1]
    barrier = pltpu.get_barrier_semaphore()

    def signal(semaphore, device):
        pl.semaphore_signal(semaphore, inc=1, device_id=device, device_id_type=MESH)

    for d in near:
        signal(barrier, along_z(d))
    for d in range(1, SEG):
        signal(barrier, along_tm(d))
    for d in range(1, NYC):
        signal(barrier, along_yc(d))

    inputs[0].wait()
    bands = tap_bands(taps)
    inputs[1].wait()
    normed = normalize(raw[0], bands)
    xall[tm] = normed.astype(bf16)

    inputs[2].wait()
    ids = jnp.concatenate([ids_ref[r : r + 1, :] for r in range(4)], 1)
    chosen = (iota((CH, SOURCES), 0) == ids - place * CH).astype(f32).astype(bf16)
    picked = lax.dot_general(chosen, xall[tm], TN, preferred_element_type=f32).astype(bf16)
    for t in range(SEG):
        for h in range(2):
            send1[t, h] = picked[ROWS * t : ROWS * (t + 1), 128 * h : 128 * (h + 1)]

    pl.semaphore_wait(barrier, len(near) + NYC - 1 + SEG - 1)

    spread = [d for d in near if d != 4]
    first = [
        pltpu.make_async_remote_copy(
            send1.at[lax.rem(z + d + NZ, SEG)], recv1.at[i], s1_send.at[i], s1_recv.at[i], along_z(d), MESH
        )
        for i, d in enumerate(spread)
    ]
    for copy in first:
        copy.start()
    signal(column, along_z(-4))
    signal(column, along_z(4))
    gather = [
        pltpu.make_async_remote_copy(
            xall.at[tm], xall.at[tm], x_send.at[d], x_recv.at[d], along_tm(d), MESH
        )
        for d in range(1, SEG)
    ]
    for copy in gather:
        copy.start()

    total = send1[owner].astype(f32)
    for i in reversed(range(len(spread))):
        first[i].wait_recv()
        total = total + recv1[i].astype(f32)
    mine2[...] = total.astype(bf16)

    second = [
        pltpu.make_async_remote_copy(
            mine2.at[core if d == 2 else 1 - core], recv2.at[d], s2_send.at[d], s2_recv.at[d], along_yc(d), MESH
        )
        for d in range(1, NYC)
    ]
    for copy in second:
        copy.start()

    pl.semaphore_wait(column, 2)

    @pl.when(own)
    def _():
        for d in range(1, SEG):
            signal(ready, along_tm(d))

    total = mine2[core].astype(f32)
    for d in range(1, NYC):
        second[d - 1].wait_recv()
        total = total + recv2[d].astype(f32)
    mine3[...] = total.astype(bf16)

    pl.when(jnp.logical_not(own))(lambda: pl.semaphore_wait(ready, 1))
    slot = 2 * tm + lax.div(z, SEG)
    third = [
        pltpu.make_async_remote_copy(
            mine3, parts.at[slot], s3_send.at[d], s3_recv.at[slot], at(owner, d, yc), MESH
        )
        for d in range(NZ)
    ]
    here = pltpu.make_async_copy(mine3, parts.at[slot], s3_recv.at[slot])
    for d in (8, 7, 9, 6, 10, 5, 11, 4, 12, 3, 13, 2, 14, 1, 15):
        third[d].start()
    pl.when(own)(lambda: here.start())
    pl.when(jnp.logical_not(own))(lambda: third[0].start())

    step = iota((SAMPLES, CH), 0)
    for g in range(SEG):
        if g:
            gather[g - 1].wait_recv()
    for g in range(SEG):
        x = xall[g].astype(f32).T
        later = jnp.where(step == SAMPLES - 1, 0.0, pltpu.roll(x, SAMPLES - 1, 0))
        earlier = jnp.where(step == 0, 0.0, pltpu.roll(x, 1, 0))
        span = slice(SAMPLES * g, SAMPLES * (g + 1))
        rhs_up[span, :CH] = x.astype(bf16)
        rhs_up[span, CH:] = later.astype(bf16)
        rhs_down[span, :CH] = x.astype(bf16)
        rhs_down[span, CH:] = earlier.astype(bf16)

    for g in range(SEG):
        for p in range(2):
            i = 2 * g + p
            pltpu.make_async_copy(parts.at[i], parts.at[i], s3_recv.at[i]).wait()
        rows[core, g] = (parts[2 * g].astype(f32) + parts[2 * g + 1].astype(f32)).astype(bf16)

    swap = pltpu.make_async_remote_copy(
        rows.at[core], rows.at[core], s4_send, s4_recv, along_yc(1), MESH
    )
    swap.start()
    swap.wait_recv()

    lane = iota((ROWS, 128), 1)
    for g in range(SEG):
        low = rows[0, g].astype(f32)
        high = rows[1, g].astype(f32)
        a, b, c = (slice(256 * g + 128 * i, 256 * g + 128 * i + 128) for i in range(3))
        for i in range(UP):
            q = 2 * i
            lo, hi = (pltpu.roll(low, q, 1), pltpu.roll(high, q, 1)) if q else (low, high)
            lhs_up[ROWS * i : ROWS * (i + 1), a] = jnp.where(lane < q, 0.0, lo).astype(bf16)
            lhs_up[ROWS * i : ROWS * (i + 1), b] = jnp.where(lane < q, lo, hi).astype(bf16)
        for i in range(DOWN):
            q = 128 - (2 * i + 1)
            lo, hi = pltpu.roll(low, q, 1), pltpu.roll(high, q, 1)
            lhs_down[ROWS * i : ROWS * (i + 1), a] = jnp.where(lane < q, lo, hi).astype(bf16)
            lhs_down[ROWS * i : ROWS * (i + 1), b] = jnp.where(lane < q, hi, 0.0).astype(bf16)

    up = jnp.dot(lhs_up[...], rhs_up[...], preferred_element_type=f32)
    for i in range(UP):
        block = (up[ROWS * i : ROWS * (i + 1)] * SCALE).astype(bf16)
        lag = MAXLAG + 2 * i
        out_ref[lag] = block[:, :CH]
        if lag + 1 < LAGS:
            out_ref[lag + 1] = block[:, CH:]
    down = jnp.dot(lhs_down[...], rhs_down[...], preferred_element_type=f32)
    for i in range(DOWN):
        block = (down[ROWS * i : ROWS * (i + 1)] * SCALE).astype(bf16)
        lag = MAXLAG - 1 - 2 * i
        out_ref[lag] = block[:, :CH]
        out_ref[lag - 1] = block[:, CH:]

    for copy in first + gather + second + third[1:] + [swap]:
        copy.wait_send()
    pl.when(jnp.logical_not(own))(lambda: third[0].wait_send())


def body(raw_strain, fir_taps, source_ids):
    hbm = pl.BlockSpec(memory_space=pltpu.HBM)
    dma = pltpu.SemaphoreType.DMA
    signals = pltpu.SemaphoreType.REGULAR
    out = pl.pallas_call(
        kernel,
        out_shape=jax.ShapeDtypeStruct((LAGS, ROWS, CH), bf16),
        in_specs=[hbm, hbm, hbm],
        out_specs=pl.BlockSpec(memory_space=pltpu.VMEM),
        scratch_shapes=[
            pltpu.VMEM((1, CH, RAW), bf16),
            pltpu.SMEM((NTAP,), f32),
            pltpu.VMEM((4, 32), jnp.int32),
            pltpu.VMEM((SEG, CH, SAMPLES), bf16),
            pltpu.VMEM((SEG, 2, ROWS, 128), bf16),
            pltpu.VMEM((7, 2, ROWS, 128), bf16),
            pltpu.VMEM((2, ROWS, 128), bf16),
            pltpu.VMEM((NYC, ROWS, 128), bf16),
            pltpu.VMEM((ROWS, 128), bf16),
            pltpu.VMEM((2 * SEG, ROWS, 128), bf16),
            pltpu.VMEM((2, SEG, ROWS, 128), bf16),
            pltpu.VMEM((ROWS * UP, SEG * SAMPLES), bf16),
            pltpu.VMEM((ROWS * DOWN, SEG * SAMPLES), bf16),
            pltpu.VMEM((SEG * SAMPLES, 2 * CH), bf16),
            pltpu.VMEM((SEG * SAMPLES, 2 * CH), bf16),
            dma((3,)),
            dma((SEG,)), dma((SEG,)),
            dma((7,)), dma((7,)),
            dma((NYC,)), dma((NYC,)),
            dma((NZ,)), dma((2 * SEG,)),
            dma, dma,
            signals, signals,
        ],
        compiler_params=pltpu.CompilerParams(
            collective_id=0, has_side_effects=True, vmem_limit_bytes=60 * 1024 * 1024
        ),
    )(raw_strain, fir_taps, source_ids)
    return out.transpose(1, 0, 2)


def solution(mesh):
    return jax.shard_map(
        body,
        mesh=mesh,
        in_specs=(P("tm", "array", None), P(), P()),
        out_specs=P("tm", None, "array"),
        check_vma=False,
    )
```

time: 45.8 us -> 38.8 us (0.85)
  the two profiles are of different devices: /device:TPU:4 before, /device:TPU:1 now
where the time goes in v2:
time: 38.8 us; the launch traced here: 38.6 us
  Pallas kernels  36.8 us (95%)
  local copies, waits for them, and re-layouts  1.78 us (5%)
    pallas_call x1, Pallas kernels, body(): pl.pallas_call(kernel, out_shape=jax.ShapeDtypeStruct((LAGS, ROWS, CH), b...  36.8 us
    unnamed x1, local copies, waits for them, and re-layouts  1.78 us

profile of v2, /device:TPU:1, one launch (start us, length us, event | category | flops | bytes accessed | tf_op | source)
XLA Modules:
  0.0 38.6 jit_solution(7816782166672910605)
XLA Ops:
  0.0 36.8 %shard_map.37 = bf16[101,16,128]{2,1,0:T(8,128)(2,1)} custom-call(bf16[1,128,1024]{2,1,0:T(8,128)(2,1)} %raw_hbm.1, f32[8]{0:T(128)} %taps_hbm.1, s32[4,32]{1,0:T(4,128)} %ids_hbm.1), custom_call_target="tpu_custom_call" | custom-call | tf_op jit(solution)/shard_map/pallas_call | solution.py:268
  36.8 1.8 %copy.5 = bf16[16,101,128]{2,0,1:T(8,128)(2,1)} copy(bf16[16,101,128]{2,0,1:T(8,128)(2,1)} %bitcast.1) | data formatting | bytes 827392

commit v3 on v2

v3 whole, which is shorter than its diff:
```python
import functools
import math

import jax
import jax.numpy as jnp
from jax import lax
from jax.experimental import pallas as pl
from jax.experimental.pallas import tpu as pltpu
from jax.sharding import PartitionSpec as P

MESH = pl.DeviceIdType.MESH
SOURCES = 128
MAXLAG = 50
WINDOW = 64
DECIM = 4
NTAP = 8
SAMPLES = 256
LAGS = 101
RAW = 1024
SEG = 8
ROWS = 16
CH = 128
NZ = 16
NYC = 4
PLACES = NZ * NYC
SUMS = 16
SIDE = PLACES // 2
UP = 26
DOWN = 25
EPSILON = 1e-05
SCALE = 1.0 / (math.sqrt(SAMPLES) * math.sqrt(SEG))

f32 = jnp.float32
bf16 = jnp.bfloat16
TN = (((0,), (0,)), ((), ()))


def iota(shape, dim):
    return lax.broadcasted_iota(jnp.int32, shape, dim)


def terms(value, count):
    parts = []
    for _ in range(count):
        part = value.astype(bf16)
        parts.append(part)
        value = value - part.astype(f32)
    return parts


def tap_bands(taps_ref):
    k = DECIM * iota((128, 128), 1) - iota((128, 128), 0)
    band = jnp.zeros((128, 128), f32)
    for tap in range(NTAP):
        band = jnp.where(k == tap, taps_ref[tap], band)
    band = jnp.concatenate([band, jnp.zeros((128, 128), f32)], 1)
    lane = iota((128, SAMPLES), 1)
    bands = []
    for tile in range(RAW // 128):
        placed = pltpu.roll(band, 32 * tile, 1) if tile else band
        if tile == RAW // 128 - 1:
            placed = jnp.where(lane < 2, 0.0, placed)
        bands.append(terms(placed, 3))
    return bands


def normalize(raw, bands):
    filtered = jnp.zeros((CH, SAMPLES), f32)
    for term in range(3):
        matrix = jnp.concatenate([band[term] for band in bands], 0)
        filtered = filtered + jnp.dot(raw, matrix, preferred_element_type=f32)
    gap = iota((SAMPLES, SAMPLES), 0) - iota((SAMPLES, SAMPLES), 1)
    window = jnp.where((gap >= -(WINDOW // 2)) & (gap < WINDOW // 2), 1.0, 0.0).astype(bf16)
    total = jnp.zeros((CH, SAMPLES), f32)
    for part in terms(jnp.abs(filtered), 2):
        total = total + jnp.dot(part, window, preferred_element_type=f32)
    return filtered / (total * (1.0 / WINDOW) + EPSILON)


def kernel(
    raw_hbm, taps_hbm, ids_hbm, out_ref,
    raw, taps, ids_ref, xall, send0, recv0, send1, recv1, mine, parts, lhs_up, lhs_down, rhs_up, rhs_down,
    in_sem, x_send, x_recv, s0_send, s0_recv, s1_send, s1_recv, s2_send, s2_recv, s3_send, s3_recv, column, ready,
):
    inputs = [
        pltpu.make_async_copy(src, dst, in_sem.at[i])
        for i, (src, dst) in enumerate(((taps_hbm, taps), (raw_hbm, raw), (ids_hbm, ids_ref)))
    ]
    for copy in inputs:
        copy.start()

    tm = lax.axis_index("tm")
    place = lax.axis_index("array")
    z = lax.div(place, NYC)
    core = lax.rem(place, 2)
    side = lax.rem(lax.div(place, 2), 2)
    other = place + 1 - 2 * core
    sums = place < SUMS
    owner = z + 4 * side

    def along_tm(d):
        return {"tm": lax.rem(tm + d, SEG), "array": place}

    def signal(semaphore, device):
        pl.semaphore_signal(semaphore, inc=1, device_id=device, device_id_type=MESH)

    barrier = pltpu.get_barrier_semaphore()
    for d in range(1, SEG):
        signal(barrier, along_tm(d))
    signal(barrier, {"tm": tm, "array": other})

    @pl.when(sums)
    def _():
        def greet(d, carry):
            signal(barrier, {"tm": tm, "array": lax.rem(place + 2 * d, PLACES)})
            return carry

        lax.fori_loop(1, SIDE, greet, 0)

    inputs[0].wait()
    bands = tap_bands(taps)
    inputs[1].wait()
    normed = normalize(raw[0], bands)
    xall[tm] = normed.astype(bf16)

    inputs[2].wait()
    ids = jnp.concatenate([ids_ref[r : r + 1, :] for r in range(4)], 1)
    chosen = (iota((CH, SOURCES), 0) == ids - place * CH).astype(f32).astype(bf16)
    picked = lax.dot_general(chosen, xall[tm], TN, preferred_element_type=f32)
    for t in range(SEG):
        for h in range(2):
            part = picked[ROWS * t + 8 * h : ROWS * t + 8 * h + 8]
            send0[h, t] = jnp.concatenate([part[:, :128], part[:, 128:]], 0).astype(bf16)

    pl.semaphore_wait(barrier, jnp.where(sums, SEG - 1, SEG) + SEG - 1 + 1)

    halves = pltpu.make_async_remote_copy(
        send0.at[1 - core], recv0, s0_send, s0_recv, {"tm": tm, "array": other}, MESH
    )
    halves.start()

    @pl.when(jnp.logical_not(sums))
    def _():
        for k in range(0, SUMS, 2):
            signal(column, {"tm": tm, "array": k + core})

    halves.wait_recv()
    for t in range(SEG):
        send1[t] = (send0[core, t].astype(f32) + recv0[t].astype(f32)).astype(bf16)

    for i in range(SEG):
        plane = jnp.where(z < 10, i // 2, 3 - i // 2)
        across = lax.rem(side + 1 + i, 2)
        k = plane * NYC + 2 * across + core
        copy = pltpu.make_async_remote_copy(
            send1.at[plane + 4 * across], recv1.at[lax.div(lax.rem(place - k + PLACES, PLACES), 2)],
            s1_send, s1_recv, {"tm": tm, "array": k}, MESH,
        )
        pl.when(place != k)(copy.start)

    gather = [
        pltpu.make_async_remote_copy(
            xall.at[tm], xall.at[tm], x_send.at[d], x_recv.at[d], along_tm(d), MESH
        )
        for d in range(1, SEG)
    ]
    for copy in gather:
        copy.start()

    @pl.when(sums)
    def _():
        pl.semaphore_wait(column, SIDE - SEG)

        @pl.when(tm == owner)
        def _():
            for d in range(1, SEG):
                signal(ready, along_tm(d))

    @pl.when(sums)
    def _():
        others = recv1.at[pl.ds(1, SIDE - 1)]
        pltpu.make_async_copy(others, others, s1_recv).wait()
        total = send1[owner].astype(f32)
        for i in range(1, SIDE):
            total = total + recv1[i].astype(f32)
        mine[...] = total.astype(bf16)
        pl.when(tm != owner)(lambda: pl.semaphore_wait(ready, 1))

        def spread(i, carry):
            p = 2 * i + core
            copy = pltpu.make_async_remote_copy(
                mine, parts.at[core, tm], s2_send, s2_recv, {"tm": owner, "array": p}, MESH
            )
            here = (tm == owner) & (p == place)
            pl.when(jnp.logical_not(here))(copy.start)
            return carry

        lax.fori_loop(0, SIDE, spread, 0)
        pl.when(tm == owner)(lambda: pltpu.make_async_copy(mine, parts.at[core, tm], s2_recv).start())

    step = iota((SAMPLES, CH), 0)
    for copy in gather:
        copy.wait_recv()
    for g in range(SEG):
        x = xall[g].astype(f32).T
        later = jnp.where(step == SAMPLES - 1, 0.0, pltpu.roll(x, SAMPLES - 1, 0))
        earlier = jnp.where(step == 0, 0.0, pltpu.roll(x, 1, 0))
        span = slice(SAMPLES * g, SAMPLES * (g + 1))
        rhs_up[span, :CH] = x.astype(bf16)
        rhs_up[span, CH:] = later.astype(bf16)
        rhs_down[span, :CH] = x.astype(bf16)
        rhs_down[span, CH:] = earlier.astype(bf16)

    pltpu.make_async_copy(parts.at[core], parts.at[core], s2_recv).wait()

    swap = pltpu.make_async_remote_copy(
        parts.at[core], parts.at[core], s3_send, s3_recv, {"tm": tm, "array": other}, MESH
    )
    swap.start()
    swap.wait_recv()

    lane = iota((ROWS, 128), 1)
    for g in range(SEG):
        one = parts[0, g].astype(f32)
        two = parts[1, g].astype(f32)
        low = jnp.concatenate([one[:8], two[:8]], 0)
        high = jnp.concatenate([one[8:], two[8:]], 0)
        a, b = slice(256 * g, 256 * g + 128), slice(256 * g + 128, 256 * g + 256)
        for i in range(UP):
            q = 2 * i
            lo, hi = (pltpu.roll(low, q, 1), pltpu.roll(high, q, 1)) if q else (low, high)
            lhs_up[ROWS * i : ROWS * (i + 1), a] = jnp.where(lane < q, 0.0, lo).astype(bf16)
            lhs_up[ROWS * i : ROWS * (i + 1), b] = jnp.where(lane < q, lo, hi).astype(bf16)
        for i in range(DOWN):
            q = 128 - (2 * i + 1)
            lo, hi = pltpu.roll(low, q, 1), pltpu.roll(high, q, 1)
            lhs_down[ROWS * i : ROWS * (i + 1), a] = jnp.where(lane < q, lo, hi).astype(bf16)
            lhs_down[ROWS * i : ROWS * (i + 1), b] = jnp.where(lane < q, hi, 0.0).astype(bf16)

    up = jnp.dot(lhs_up[...], rhs_up[...], preferred_element_type=f32)
    for i in range(UP):
        block = (up[ROWS * i : ROWS * (i + 1)] * SCALE).astype(bf16)
        lag = MAXLAG + 2 * i
        out_ref[lag] = block[:, :CH]
        if lag + 1 < LAGS:
            out_ref[lag + 1] = block[:, CH:]
    down = jnp.dot(lhs_down[...], rhs_down[...], preferred_element_type=f32)
    for i in range(DOWN):
        block = (down[ROWS * i : ROWS * (i + 1)] * SCALE).astype(bf16)
        lag = MAXLAG - 1 - 2 * i
        out_ref[lag] = block[:, :CH]
        out_ref[lag - 1] = block[:, CH:]

    for copy in gather + [halves, swap]:
        copy.wait_send()

    @pl.when(jnp.logical_not(sums))
    def _():
        pltpu.make_async_copy(send1, send1, s1_send).wait()

    @pl.when(sums)
    def _():
        fewer = send1.at[pl.ds(1, SEG - 1)]
        pltpu.make_async_copy(fewer, fewer, s1_send).wait()
        others = recv1.at[pl.ds(1, SIDE - 1)]
        pl.when(tm != owner)(lambda: pltpu.make_async_copy(recv1, recv1, s2_send).wait())
        pl.when(tm == owner)(lambda: pltpu.make_async_copy(others, others, s2_send).wait())


def body(raw_strain, fir_taps, source_ids):
    hbm = pl.BlockSpec(memory_space=pltpu.HBM)
    dma = pltpu.SemaphoreType.DMA
    signals = pltpu.SemaphoreType.REGULAR
    out = pl.pallas_call(
        kernel,
        out_shape=jax.ShapeDtypeStruct((LAGS, ROWS, CH), bf16),
        in_specs=[hbm, hbm, hbm],
        out_specs=pl.BlockSpec(memory_space=pltpu.VMEM),
        scratch_shapes=[
            pltpu.VMEM((1, CH, RAW), bf16),
            pltpu.SMEM((NTAP,), f32),
            pltpu.VMEM((4, 32), jnp.int32),
            pltpu.VMEM((SEG, CH, SAMPLES), bf16),
            pltpu.VMEM((2, SEG, 16, 128), bf16),
            pltpu.VMEM((SEG, 16, 128), bf16),
            pltpu.VMEM((SEG, 16, 128), bf16),
            pltpu.VMEM((SIDE, 16, 128), bf16),
            pltpu.VMEM((16, 128), bf16),
            pltpu.VMEM((2, SEG, 16, 128), bf16),
            pltpu.VMEM((ROWS * UP, SEG * SAMPLES), bf16),
            pltpu.VMEM((ROWS * DOWN, SEG * SAMPLES), bf16),
            pltpu.VMEM((SEG * SAMPLES, 2 * CH), bf16),
            pltpu.VMEM((SEG * SAMPLES, 2 * CH), bf16),
            dma((3,)),
            dma((SEG,)), dma((SEG,)),
            dma, dma,
            dma, dma,
            dma, dma,
            dma, dma,
            signals, signals,
        ],
        compiler_params=pltpu.CompilerParams(
            collective_id=0, has_side_effects=True, vmem_limit_bytes=60 * 1024 * 1024
        ),
    )(raw_strain, fir_taps, source_ids)
    return out.transpose(1, 0, 2)


def solution(mesh):
    return jax.shard_map(
        body,
        mesh=mesh,
        in_specs=(P("tm", "array", None), P(), P()),
        out_specs=P("tm", None, "array"),
        check_vma=False,
    )
```

time: 38.8 us -> 34.5 us (0.89)
  Pallas kernels: 36.8 us -> 32.5 us
    pallas_call x1, Pallas kernels: 36.8 us -> 32.5 us  [body(): pl.pallas_call(kernel, out_shape=jax.ShapeDtypeStruct((LAGS, ROWS, CH), b...]
where the time goes in v3:
time: 34.5 us; the launch traced here: 34.3 us
  Pallas kernels  32.5 us (94%)
  local copies, waits for them, and re-layouts  1.78 us (5%)
    pallas_call x1, Pallas kernels, body(): pl.pallas_call(kernel, out_shape=jax.ShapeDtypeStruct((LAGS, ROWS, CH), b...  32.5 us
    unnamed x1, local copies, waits for them, and re-layouts  1.78 us

profile of v3, /device:TPU:1, one launch (start us, length us, event | category | flops | bytes accessed | tf_op | source)
XLA Modules:
  0.0 34.3 jit_solution(11575034103716140592)
XLA Ops:
  0.0 32.5 %shard_map.37 = bf16[101,16,128]{2,1,0:T(8,128)(2,1)} custom-call(bf16[1,128,1024]{2,1,0:T(8,128)(2,1)} %raw_hbm.1, f32[8]{0:T(128)} %taps_hbm.1, s32[4,32]{1,0:T(4,128)} %ids_hbm.1), custom_call_target="tpu_custom_call" | custom-call | tf_op jit(solution)/shard_map/pallas_call | solution.py:274
  32.5 1.8 %copy.5 = bf16[16,101,128]{2,0,1:T(8,128)(2,1)} copy(bf16[16,101,128]{2,0,1:T(8,128)(2,1)} %bitcast.1) | data formatting | bytes 827392

commit v4 on v3

--- a/solution.py
+++ b/solution.py
@@ -25,6 +25,7 @@
 PLACES = NZ * NYC
 SUMS = 16
 SIDE = PLACES // 2
+USERS = SUMS + (PLACES - SUMS) // 2
 UP = 26
 DOWN = 25
 EPSILON = 1e-05
@@ -80,7 +81,7 @@
 def kernel(
     raw_hbm, taps_hbm, ids_hbm, out_ref,
     raw, taps, ids_ref, xall, send0, recv0, send1, recv1, mine, parts, lhs_up, lhs_down, rhs_up, rhs_down,
-    in_sem, x_send, x_recv, s0_send, s0_recv, s1_send, s1_recv, s2_send, s2_recv, s3_send, s3_recv, column, ready,
+    in_sem, x_send, x_recv, s0_send, s0_recv, s1_send, s1_recv, s2_send, s2_recv, s3_send, s3_recv, column, beside, beyond, ready,
 ):
     inputs = [
         pltpu.make_async_copy(src, dst, in_sem.at[i])
@@ -98,16 +99,19 @@
     sums = place < SUMS
     owner = z + 4 * side
 
-    def along_tm(d):
-        return {"tm": lax.rem(tm + d, SEG), "array": place}
+    right, left = lax.rem(tm + 2, SEG), lax.rem(tm + 6, SEG)
+    across = tm + 1 - 2 * lax.rem(tm, 2)
+
+    def in_tm(t):
+        return {"tm": t, "array": place}
 
     def signal(semaphore, device):
         pl.semaphore_signal(semaphore, inc=1, device_id=device, device_id_type=MESH)
 
     barrier = pltpu.get_barrier_semaphore()
-    for d in range(1, SEG):
-        signal(barrier, along_tm(d))
-    signal(barrier, {"tm": tm, "array": other})
+    for t in (across, left, right):
+        signal(barrier, in_tm(t))
+    pl.when(jnp.logical_not(sums))(lambda: signal(barrier, {"tm": tm, "array": other}))
 
     @pl.when(sums)
     def _():
@@ -115,10 +119,23 @@
             signal(barrier, {"tm": tm, "array": lax.rem(place + 2 * d, PLACES)})
             return carry
 
+        for k in range(0, SUMS, 2):
+            signal(barrier, {"tm": tm, "array": k + 1 - core})
         lax.fori_loop(1, SIDE, greet, 0)
 
     inputs[0].wait()
     bands = tap_bands(taps)
+
+    pl.semaphore_wait(barrier, jnp.where(sums, SUMS - 1, SEG + 1) + 3)
+
+    @pl.when(jnp.logical_not(sums))
+    def _():
+        for k in range(0, SUMS, 2):
+            signal(column, {"tm": tm, "array": k + core})
+
+    signal(beside, in_tm(left))
+    signal(beside, in_tm(across))
+
     inputs[1].wait()
     normed = normalize(raw[0], bands)
     xall[tm] = normed.astype(bf16)
@@ -132,17 +149,14 @@
             part = picked[ROWS * t + 8 * h : ROWS * t + 8 * h + 8]
             send0[h, t] = jnp.concatenate([part[:, :128], part[:, 128:]], 0).astype(bf16)
 
-    pl.semaphore_wait(barrier, jnp.where(sums, SEG - 1, SEG) + SEG - 1 + 1)
-
     halves = pltpu.make_async_remote_copy(
         send0.at[1 - core], recv0, s0_send, s0_recv, {"tm": tm, "array": other}, MESH
     )
     halves.start()
 
-    @pl.when(jnp.logical_not(sums))
-    def _():
-        for k in range(0, SUMS, 2):
-            signal(column, {"tm": tm, "array": k + core})
+    pl.semaphore_wait(beside, 2)
+    signal(beyond, in_tm(across))
+
 
     halves.wait_recv()
     for t in range(SEG):
@@ -150,17 +164,18 @@
 
     for i in range(SEG):
         plane = jnp.where(z < 10, i // 2, 3 - i // 2)
-        across = lax.rem(side + 1 + i, 2)
-        k = plane * NYC + 2 * across + core
+        to_side = lax.rem(side + 1 + i, 2)
+        k = plane * NYC + 2 * to_side + core
         copy = pltpu.make_async_remote_copy(
-            send1.at[plane + 4 * across], recv1.at[lax.div(lax.rem(place - k + PLACES, PLACES), 2)],
+            send1.at[plane + 4 * to_side], recv1.at[lax.div(lax.rem(place - k + PLACES, PLACES), 2)],
             s1_send, s1_recv, {"tm": tm, "array": k}, MESH,
         )
         pl.when(place != k)(copy.start)
 
+    pl.semaphore_wait(beyond, 1)
     gather = [
         pltpu.make_async_remote_copy(
-            xall.at[tm], xall.at[tm], x_send.at[d], x_recv.at[d], along_tm(d), MESH
+            xall.at[tm], xall.at[tm], x_send.at[d], x_recv.at[d], in_tm(lax.rem(tm + d, SEG)), MESH
         )
         for d in range(1, SEG)
     ]
@@ -174,7 +189,7 @@
         @pl.when(tm == owner)
         def _():
             for d in range(1, SEG):
-                signal(ready, along_tm(d))
+                signal(ready, in_tm(lax.rem(tm + d, SEG)))
 
     @pl.when(sums)
     def _():
@@ -187,7 +202,7 @@
         pl.when(tm != owner)(lambda: pl.semaphore_wait(ready, 1))
 
         def spread(i, carry):
-            p = 2 * i + core
+            p = jnp.where(i < SUMS, i, 2 * i - SUMS + core)
             copy = pltpu.make_async_remote_copy(
                 mine, parts.at[core, tm], s2_send, s2_recv, {"tm": owner, "array": p}, MESH
             )
@@ -195,7 +210,7 @@
             pl.when(jnp.logical_not(here))(copy.start)
             return carry
 
-        lax.fori_loop(0, SIDE, spread, 0)
+        lax.fori_loop(0, USERS, spread, 0)
         pl.when(tm == owner)(lambda: pltpu.make_async_copy(mine, parts.at[core, tm], s2_recv).start())
 
     step = iota((SAMPLES, CH), 0)
@@ -211,13 +226,16 @@
         rhs_down[span, :CH] = x.astype(bf16)
         rhs_down[span, CH:] = earlier.astype(bf16)
 
-    pltpu.make_async_copy(parts.at[core], parts.at[core], s2_recv).wait()
-
     swap = pltpu.make_async_remote_copy(
         parts.at[core], parts.at[core], s3_send, s3_recv, {"tm": tm, "array": other}, MESH
     )
-    swap.start()
-    swap.wait_recv()
+    pl.when(sums)(lambda: pltpu.make_async_copy(parts, parts, s2_recv).wait())
+
+    @pl.when(jnp.logical_not(sums))
+    def _():
+        pltpu.make_async_copy(parts.at[core], parts.at[core], s2_recv).wait()
+        swap.start()
+        swap.wait_recv()
 
     lane = iota((ROWS, 128), 1)
     for g in range(SEG):
@@ -251,18 +269,19 @@
         out_ref[lag] = block[:, :CH]
         out_ref[lag - 1] = block[:, CH:]
 
-    for copy in gather + [halves, swap]:
+    for copy in gather + [halves]:
         copy.wait_send()
 
     @pl.when(jnp.logical_not(sums))
     def _():
+        swap.wait_send()
         pltpu.make_async_copy(send1, send1, s1_send).wait()
 
     @pl.when(sums)
     def _():
         fewer = send1.at[pl.ds(1, SEG - 1)]
         pltpu.make_async_copy(fewer, fewer, s1_send).wait()
-        others = recv1.at[pl.ds(1, SIDE - 1)]
+        others = recv1.at[pl.ds(1, USERS - 1)]
         pl.when(tm != owner)(lambda: pltpu.make_async_copy(recv1, recv1, s2_send).wait())
         pl.when(tm == owner)(lambda: pltpu.make_async_copy(others, others, s2_send).wait())
 
@@ -273,7 +292,7 @@
     signals = pltpu.SemaphoreType.REGULAR
     out = pl.pallas_call(
         kernel,
-        out_shape=jax.ShapeDtypeStruct((LAGS, ROWS, CH), bf16),
+        out_shape=pltpu.VMEM((LAGS, ROWS, CH), bf16),
         in_specs=[hbm, hbm, hbm],
         out_specs=pl.BlockSpec(memory_space=pltpu.VMEM),
         scratch_shapes=[
@@ -284,7 +303,7 @@
             pltpu.VMEM((2, SEG, 16, 128), bf16),
             pltpu.VMEM((SEG, 16, 128), bf16),
             pltpu.VMEM((SEG, 16, 128), bf16),
-            pltpu.VMEM((SIDE, 16, 128), bf16),
+            pltpu.VMEM((USERS, 16, 128), bf16),
             pltpu.VMEM((16, 128), bf16),
             pltpu.VMEM((2, SEG, 16, 128), bf16),
             pltpu.VMEM((ROWS * UP, SEG * SAMPLES), bf16),
@@ -297,10 +316,10 @@
             dma, dma,
             dma, dma,
             dma, dma,
-            signals, signals,
+            signals, signals, signals, signals,
         ],
         compiler_params=pltpu.CompilerParams(
-            collective_id=0, has_side_effects=True, vmem_limit_bytes=60 * 1024 * 1024
+            collective_id=0, has_side_effects=True, vmem_limit_bytes=56 * 1024 * 1024
         ),
     )(raw_strain, fir_taps, source_ids)
     return out.transpose(1, 0, 2)

time: 34.5 us -> 31.4 us (0.910)
  Pallas kernels: 32.5 us -> 30.5 us
  local copies, waits for them, and re-layouts: 1.78 us -> 0.76 us
    pallas_call x1, Pallas kernels: 32.5 us -> 30.5 us  [body(): pl.pallas_call(kernel, out_shape=pltpu.VMEM((LAGS, ROWS, CH), bf16), in_s...]
    unnamed x1, local copies, waits for them, and re-layouts: 1.78 us -> 0.76 us
where the time goes in v4:
time: 31.4 us; the launch traced here: 31.3 us
  Pallas kernels  30.5 us (97%)
  local copies, waits for them, and re-layouts  0.76 us (2%)
    pallas_call x1, Pallas kernels, body(): pl.pallas_call(kernel, out_shape=pltpu.VMEM((LAGS, ROWS, CH), bf16), in_s...  30.5 us
    unnamed x1, local copies, waits for them, and re-layouts  0.76 us

profile of v4, /device:TPU:1, one launch (start us, length us, event | category | flops | bytes accessed | tf_op | source)
XLA Modules:
  0.0 31.3 jit_solution(11983723552772032617)
XLA Ops:
  0.0 30.5 %shard_map.37 = bf16[101,16,128]{2,1,0:T(8,128)(2,1)S(1)} custom-call(bf16[1,128,1024]{2,1,0:T(8,128)(2,1)} %raw_hbm.1, f32[8]{0:T(128)} %taps_hbm.1, s32[4,32]{1,0:T(4,128)} %ids_hbm.1), custom_call_target="tpu_custom_call" | custom-call | tf_op jit(solution)/shard_map/pallas_call | solution.py:293
  30.5 0.8 %copy.5 = bf16[16,101,128]{2,0,1:T(8,128)(2,1)} copy(bf16[16,101,128]{2,0,1:T(8,128)(2,1)S(1)} %bitcast.1) | data formatting | bytes 827392

commit v5 on v4

--- a/solution.py
+++ b/solution.py
@@ -25,6 +25,7 @@
 PLACES = NZ * NYC
 SUMS = 16
 SIDE = PLACES // 2
+AWAIT = {0: 4, 4: 8}
 USERS = SUMS + (PLACES - SUMS) // 2
 UP = 26
 DOWN = 25
@@ -65,11 +66,15 @@
     return bands
 
 
-def normalize(raw, bands):
+def decimate(raw, bands):
     filtered = jnp.zeros((CH, SAMPLES), f32)
     for term in range(3):
         matrix = jnp.concatenate([band[term] for band in bands], 0)
         filtered = filtered + jnp.dot(raw, matrix, preferred_element_type=f32)
+    return filtered
+
+
+def normalize(filtered):
     gap = iota((SAMPLES, SAMPLES), 0) - iota((SAMPLES, SAMPLES), 1)
     window = jnp.where((gap >= -(WINDOW // 2)) & (gap < WINDOW // 2), 1.0, 0.0).astype(bf16)
     total = jnp.zeros((CH, SAMPLES), f32)
@@ -80,8 +85,8 @@
 
 def kernel(
     raw_hbm, taps_hbm, ids_hbm, out_ref,
-    raw, taps, ids_ref, xall, send0, recv0, send1, recv1, mine, parts, lhs_up, lhs_down, rhs_up, rhs_down,
-    in_sem, x_send, x_recv, s0_send, s0_recv, s1_send, s1_recv, s2_send, s2_recv, s3_send, s3_recv, column, beside, beyond, ready,
+    raw, taps, ids_ref, xall, send0, recv0, send1, recv1, mine, parts, rhs_up, rhs_down,
+    in_sem, x_send, x_recv, s0_send, s0_recv, s1_send, s1_recv, s2_send, s2_recv, s3_send, s3_recv, column, beside, beyond, ready, complete,
 ):
     inputs = [
         pltpu.make_async_copy(src, dst, in_sem.at[i])
@@ -126,6 +131,9 @@
     inputs[0].wait()
     bands = tap_bands(taps)
 
+    inputs[1].wait()
+    filtered = decimate(raw[0], bands)
+
     pl.semaphore_wait(barrier, jnp.where(sums, SUMS - 1, SEG + 1) + 3)
 
     @pl.when(jnp.logical_not(sums))
@@ -136,9 +144,7 @@
     signal(beside, in_tm(left))
     signal(beside, in_tm(across))
 
-    inputs[1].wait()
-    normed = normalize(raw[0], bands)
-    xall[tm] = normed.astype(bf16)
+    xall[tm] = normalize(filtered).astype(bf16)
 
     inputs[2].wait()
     ids = jnp.concatenate([ids_ref[r : r + 1, :] for r in range(4)], 1)
@@ -182,14 +188,15 @@
     for copy in gather:
         copy.start()
 
+    def announce(semaphore):
+        for d in range(1, SEG):
+            signal(semaphore, in_tm(lax.rem(tm + d, SEG)))
+
     @pl.when(sums)
     def _():
+        pl.when(tm == owner)(lambda: announce(ready))
         pl.semaphore_wait(column, SIDE - SEG)
-
-        @pl.when(tm == owner)
-        def _():
-            for d in range(1, SEG):
-                signal(ready, in_tm(lax.rem(tm + d, SEG)))
+        pl.when(tm == owner)(lambda: announce(complete))
 
     @pl.when(sums)
     def _():
@@ -201,17 +208,23 @@
         mine[...] = total.astype(bf16)
         pl.when(tm != owner)(lambda: pl.semaphore_wait(ready, 1))
 
-        def spread(i, carry):
-            p = jnp.where(i < SUMS, i, 2 * i - SUMS + core)
+        def spread(p):
             copy = pltpu.make_async_remote_copy(
-                mine, parts.at[core, tm], s2_send, s2_recv, {"tm": owner, "array": p}, MESH
+                mine, parts.at[core, tm], s2_send, s2_recv.at[tm], {"tm": owner, "array": p}, MESH
             )
-            here = (tm == owner) & (p == place)
-            pl.when(jnp.logical_not(here))(copy.start)
+            pl.when(jnp.logical_not((tm == owner) & (p == place)))(copy.start)
+
+        for p in range(0, SUMS, 2):
+            spread(p + 1)
+            spread(p)
+        pl.when(tm != owner)(lambda: pl.semaphore_wait(complete, 1))
+
+        def one_side(i, carry):
+            spread(2 * i + core)
             return carry
 
-        lax.fori_loop(0, USERS, spread, 0)
-        pl.when(tm == owner)(lambda: pltpu.make_async_copy(mine, parts.at[core, tm], s2_recv).start())
+        lax.fori_loop(SUMS // 2, SIDE, one_side, 0)
+        pl.when(tm == owner)(lambda: pltpu.make_async_copy(mine, parts.at[core, tm], s2_recv.at[tm]).start())
 
     step = iota((SAMPLES, CH), 0)
     for copy in gather:
@@ -220,51 +233,60 @@
         x = xall[g].astype(f32).T
         later = jnp.where(step == SAMPLES - 1, 0.0, pltpu.roll(x, SAMPLES - 1, 0))
         earlier = jnp.where(step == 0, 0.0, pltpu.roll(x, 1, 0))
-        span = slice(SAMPLES * g, SAMPLES * (g + 1))
-        rhs_up[span, :CH] = x.astype(bf16)
-        rhs_up[span, CH:] = later.astype(bf16)
-        rhs_down[span, :CH] = x.astype(bf16)
-        rhs_down[span, CH:] = earlier.astype(bf16)
+        rhs_up[g, :, :CH] = x.astype(bf16)
+        rhs_up[g, :, CH:] = later.astype(bf16)
+        rhs_down[g, :, :CH] = x.astype(bf16)
+        rhs_down[g, :, CH:] = earlier.astype(bf16)
 
     swap = pltpu.make_async_remote_copy(
         parts.at[core], parts.at[core], s3_send, s3_recv, {"tm": tm, "array": other}, MESH
     )
-    pl.when(sums)(lambda: pltpu.make_async_copy(parts, parts, s2_recv).wait())
 
     @pl.when(jnp.logical_not(sums))
     def _():
-        pltpu.make_async_copy(parts.at[core], parts.at[core], s2_recv).wait()
+        for g in range(SEG):
+            pltpu.make_async_copy(mine, mine, s2_recv.at[g]).wait()
         swap.start()
         swap.wait_recv()
 
     lane = iota((ROWS, 128), 1)
-    for g in range(SEG):
+    none = jnp.zeros((ROWS, 128), bf16)
+    rising = jnp.zeros((ROWS * UP, 2 * CH), f32)
+    falling = jnp.zeros((ROWS * DOWN, 2 * CH), f32)
+    order = [lax.rem(g, SEG) for g in (tm, right, left, across, tm + 4, across + 2, across + 6, across + 4)]
+    pair = send1.at[pl.ds(0, 2)]
+    for i, g in enumerate(order):
+        if i in AWAIT:
+
+            @pl.when(sums)
+            def _():
+                for j in range(i, AWAIT[i]):
+                    pltpu.make_async_copy(pair, pair, s2_recv.at[order[j]]).wait()
+
         one = parts[0, g].astype(f32)
         two = parts[1, g].astype(f32)
-        low = jnp.concatenate([one[:8], two[:8]], 0)
-        high = jnp.concatenate([one[8:], two[8:]], 0)
-        a, b = slice(256 * g, 256 * g + 128), slice(256 * g + 128, 256 * g + 256)
+        low = jnp.concatenate([one[:8], two[:8]], 0).astype(bf16)
+        high = jnp.concatenate([one[8:], two[8:]], 0).astype(bf16)
+        later, earlier = [], []
         for i in range(UP):
             q = 2 * i
             lo, hi = (pltpu.roll(low, q, 1), pltpu.roll(high, q, 1)) if q else (low, high)
-            lhs_up[ROWS * i : ROWS * (i + 1), a] = jnp.where(lane < q, 0.0, lo).astype(bf16)
-            lhs_up[ROWS * i : ROWS * (i + 1), b] = jnp.where(lane < q, lo, hi).astype(bf16)
+            later.append(jnp.concatenate([jnp.where(lane < q, none, lo), jnp.where(lane < q, lo, hi)], 1))
         for i in range(DOWN):
             q = 128 - (2 * i + 1)
             lo, hi = pltpu.roll(low, q, 1), pltpu.roll(high, q, 1)
-            lhs_down[ROWS * i : ROWS * (i + 1), a] = jnp.where(lane < q, lo, hi).astype(bf16)
-            lhs_down[ROWS * i : ROWS * (i + 1), b] = jnp.where(lane < q, hi, 0.0).astype(bf16)
-
-    up = jnp.dot(lhs_up[...], rhs_up[...], preferred_element_type=f32)
+            earlier.append(jnp.concatenate([jnp.where(lane < q, lo, hi), jnp.where(lane < q, hi, none)], 1))
+        rising = rising + jnp.dot(jnp.concatenate(later, 0), rhs_up[g], preferred_element_type=f32)
+        falling = falling + jnp.dot(jnp.concatenate(earlier, 0), rhs_down[g], preferred_element_type=f32)
+
     for i in range(UP):
-        block = (up[ROWS * i : ROWS * (i + 1)] * SCALE).astype(bf16)
+        block = (rising[ROWS * i : ROWS * (i + 1)] * SCALE).astype(bf16)
         lag = MAXLAG + 2 * i
         out_ref[lag] = block[:, :CH]
         if lag + 1 < LAGS:
             out_ref[lag + 1] = block[:, CH:]
-    down = jnp.dot(lhs_down[...], rhs_down[...], preferred_element_type=f32)
     for i in range(DOWN):
-        block = (down[ROWS * i : ROWS * (i + 1)] * SCALE).astype(bf16)
+        block = (falling[ROWS * i : ROWS * (i + 1)] * SCALE).astype(bf16)
         lag = MAXLAG - 1 - 2 * i
         out_ref[lag] = block[:, :CH]
         out_ref[lag - 1] = block[:, CH:]
@@ -272,9 +294,10 @@
     for copy in gather + [halves]:
         copy.wait_send()
 
+    pl.when(jnp.logical_not(sums))(swap.wait_send)
+
     @pl.when(jnp.logical_not(sums))
     def _():
-        swap.wait_send()
         pltpu.make_async_copy(send1, send1, s1_send).wait()
 
     @pl.when(sums)
@@ -306,17 +329,15 @@
             pltpu.VMEM((USERS, 16, 128), bf16),
             pltpu.VMEM((16, 128), bf16),
             pltpu.VMEM((2, SEG, 16, 128), bf16),
-            pltpu.VMEM((ROWS * UP, SEG * SAMPLES), bf16),
-            pltpu.VMEM((ROWS * DOWN, SEG * SAMPLES), bf16),
-            pltpu.VMEM((SEG * SAMPLES, 2 * CH), bf16),
-            pltpu.VMEM((SEG * SAMPLES, 2 * CH), bf16),
+            pltpu.VMEM((SEG, SAMPLES, 2 * CH), bf16),
+            pltpu.VMEM((SEG, SAMPLES, 2 * CH), bf16),
             dma((3,)),
             dma((SEG,)), dma((SEG,)),
             dma, dma,
             dma, dma,
+            dma, dma((SEG,)),
             dma, dma,
-            dma, dma,
-            signals, signals, signals, signals,
+            signals, signals, signals, signals, signals,
         ],
         compiler_params=pltpu.CompilerParams(
             collective_id=0, has_side_effects=True, vmem_limit_bytes=56 * 1024 * 1024

time: 31.4 us -> 30.6 us (0.975)
  Pallas kernels: 30.5 us -> 29.7 us
    pallas_call x1, Pallas kernels: 30.5 us -> 29.7 us  [body(): pl.pallas_call(kernel, out_shape=pltpu.VMEM((LAGS, ROWS, CH), bf16), in_s...]
where the time goes in v5:
time: 30.6 us; the launch traced here: 30.5 us
  Pallas kernels  29.7 us (97%)
  local copies, waits for them, and re-layouts  0.76 us (2%)
    pallas_call x1, Pallas kernels, body(): pl.pallas_call(kernel, out_shape=pltpu.VMEM((LAGS, ROWS, CH), bf16), in_s...  29.7 us
    unnamed x1, local copies, waits for them, and re-layouts  0.76 us

profile of v5, /device:TPU:1, one launch (start us, length us, event | category | flops | bytes accessed | tf_op | source)
XLA Modules:
  0.0 30.5 jit_solution(7959304453837430182)
XLA Ops:
  0.0 29.7 %shard_map.37 = bf16[101,16,128]{2,1,0:T(8,128)(2,1)S(1)} custom-call(bf16[1,128,1024]{2,1,0:T(8,128)(2,1)} %raw_hbm.1, f32[8]{0:T(128)} %taps_hbm.1, s32[4,32]{1,0:T(4,128)} %ids_hbm.1), custom_call_target="tpu_custom_call" | custom-call | tf_op jit(solution)/shard_map/pallas_call | solution.py:316
  29.7 0.8 %copy.5 = bf16[16,101,128]{2,0,1:T(8,128)(2,1)} copy(bf16[16,101,128]{2,0,1:T(8,128)(2,1)S(1)} %bitcast.1) | data formatting | bytes 827392

commit v6 on v5

--- a/solution.py
+++ b/solution.py
@@ -102,20 +102,27 @@
     side = lax.rem(lax.div(place, 2), 2)
     other = place + 1 - 2 * core
     sums = place < SUMS
-    owner = z + 4 * side
+    owner = 2 * z + 1 - side
 
     right, left = lax.rem(tm + 2, SEG), lax.rem(tm + 6, SEG)
     across = tm + 1 - 2 * lax.rem(tm, 2)
 
+    beyond_side = place + 2 - 4 * side
+
     def in_tm(t):
         return {"tm": t, "array": place}
 
+    def next_along_y(t):
+        return {"tm": t, "array": beyond_side}
+
     def signal(semaphore, device):
         pl.semaphore_signal(semaphore, inc=1, device_id=device, device_id_type=MESH)
 
     barrier = pltpu.get_barrier_semaphore()
-    for t in (across, left, right):
+    for t in (left, right):
         signal(barrier, in_tm(t))
+    for t in (tm, across):
+        signal(barrier, next_along_y(t))
     pl.when(jnp.logical_not(sums))(lambda: signal(barrier, {"tm": tm, "array": other}))
 
     @pl.when(sums)
@@ -134,7 +141,7 @@
     inputs[1].wait()
     filtered = decimate(raw[0], bands)
 
-    pl.semaphore_wait(barrier, jnp.where(sums, SUMS - 1, SEG + 1) + 3)
+    pl.semaphore_wait(barrier, jnp.where(sums, SUMS - 1, SEG + 1) + 4)
 
     @pl.when(jnp.logical_not(sums))
     def _():
@@ -142,7 +149,8 @@
             signal(column, {"tm": tm, "array": k + core})
 
     signal(beside, in_tm(left))
-    signal(beside, in_tm(across))
+    signal(beside, next_along_y(tm))
+    signal(beside, next_along_y(across))
 
     xall[tm] = normalize(filtered).astype(bf16)
 
@@ -160,7 +168,7 @@
     )
     halves.start()
 
-    pl.semaphore_wait(beside, 2)
+    pl.semaphore_wait(beside, 3)
     signal(beyond, in_tm(across))
 
 
@@ -173,7 +181,7 @@
         to_side = lax.rem(side + 1 + i, 2)
         k = plane * NYC + 2 * to_side + core
         copy = pltpu.make_async_remote_copy(
-            send1.at[plane + 4 * to_side], recv1.at[lax.div(lax.rem(place - k + PLACES, PLACES), 2)],
+            send1.at[2 * plane + 1 - to_side], recv1.at[lax.div(lax.rem(place - k + PLACES, PLACES), 2)],
             s1_send, s1_recv, {"tm": tm, "array": k}, MESH,
         )
         pl.when(place != k)(copy.start)

time: 30.6 us -> 29.7 us (0.971)
  Pallas kernels: 29.7 us -> 28.8 us
    pallas_call x1, Pallas kernels: 29.7 us -> 28.8 us  [body(): pl.pallas_call(kernel, out_shape=pltpu.VMEM((LAGS, ROWS, CH), bf16), in_s...]
where the time goes in v6:
time: 29.7 us; the launch traced here: 29.6 us
  Pallas kernels  28.8 us (97%)
  local copies, waits for them, and re-layouts  0.76 us (3%)
    pallas_call x1, Pallas kernels, body(): pl.pallas_call(kernel, out_shape=pltpu.VMEM((LAGS, ROWS, CH), bf16), in_s...  28.8 us
    unnamed x1, local copies, waits for them, and re-layouts  0.76 us

profile of v6, /device:TPU:1, one launch (start us, length us, event | category | flops | bytes accessed | tf_op | source)
XLA Modules:
  0.0 29.6 jit_solution(548912192908851777)
XLA Ops:
  0.0 28.8 %shard_map.37 = bf16[101,16,128]{2,1,0:T(8,128)(2,1)S(1)} custom-call(bf16[1,128,1024]{2,1,0:T(8,128)(2,1)} %raw_hbm.1, f32[8]{0:T(128)} %taps_hbm.1, s32[4,32]{1,0:T(4,128)} %ids_hbm.1), custom_call_target="tpu_custom_call" | custom-call | tf_op jit(solution)/shard_map/pallas_call | solution.py:324
  28.9 0.8 %copy.5 = bf16[16,101,128]{2,0,1:T(8,128)(2,1)} copy(bf16[16,101,128]{2,0,1:T(8,128)(2,1)S(1)} %bitcast.1) | data formatting | bytes 827392

commit v7 on v6

--- a/solution.py
+++ b/solution.py
@@ -25,6 +25,7 @@
 PLACES = NZ * NYC
 SUMS = 16
 SIDE = PLACES // 2
+ORDER = (0, 1, 4, 5, 2, 3, 6, 10, 7, 9, 8, 11, 12, 13, 14, 15)
 AWAIT = {0: 4, 4: 8}
 USERS = SUMS + (PLACES - SUMS) // 2
 UP = 26
@@ -74,9 +75,12 @@
     return filtered
 
 
-def normalize(filtered):
+def window_matrix():
     gap = iota((SAMPLES, SAMPLES), 0) - iota((SAMPLES, SAMPLES), 1)
-    window = jnp.where((gap >= -(WINDOW // 2)) & (gap < WINDOW // 2), 1.0, 0.0).astype(bf16)
+    return jnp.where((gap >= -(WINDOW // 2)) & (gap < WINDOW // 2), 1.0, 0.0).astype(bf16)
+
+
+def normalize(filtered, window):
     total = jnp.zeros((CH, SAMPLES), f32)
     for part in terms(jnp.abs(filtered), 2):
         total = total + jnp.dot(part, window, preferred_element_type=f32)
@@ -90,7 +94,7 @@
 ):
     inputs = [
         pltpu.make_async_copy(src, dst, in_sem.at[i])
-        for i, (src, dst) in enumerate(((taps_hbm, taps), (raw_hbm, raw), (ids_hbm, ids_ref)))
+        for i, (src, dst) in enumerate(((raw_hbm, raw), (taps_hbm, taps), (ids_hbm, ids_ref)))
     ]
     for copy in inputs:
         copy.start()
@@ -135,28 +139,25 @@
             signal(barrier, {"tm": tm, "array": k + 1 - core})
         lax.fori_loop(1, SIDE, greet, 0)
 
-    inputs[0].wait()
+    inputs[1].wait()
     bands = tap_bands(taps)
 
-    inputs[1].wait()
-    filtered = decimate(raw[0], bands)
-
-    pl.semaphore_wait(barrier, jnp.where(sums, SUMS - 1, SEG + 1) + 4)
-
-    @pl.when(jnp.logical_not(sums))
-    def _():
-        for k in range(0, SUMS, 2):
-            signal(column, {"tm": tm, "array": k + core})
-
-    signal(beside, in_tm(left))
-    signal(beside, next_along_y(tm))
-    signal(beside, next_along_y(across))
-
-    xall[tm] = normalize(filtered).astype(bf16)
+    window = window_matrix()
 
     inputs[2].wait()
     ids = jnp.concatenate([ids_ref[r : r + 1, :] for r in range(4)], 1)
     chosen = (iota((CH, SOURCES), 0) == ids - place * CH).astype(f32).astype(bf16)
+
+    inputs[0].wait()
+    filtered = decimate(raw[0], bands)
+
+    pl.semaphore_wait(barrier, jnp.where(sums, SUMS - 1, SEG + 1) + 4)
+
+    mine_at = lax.div(tm, 2) * NYC + 2 * (1 - lax.rem(tm, 2)) + core
+    pl.when(jnp.logical_not(sums))(lambda: signal(column, {"tm": tm, "array": mine_at}))
+
+    xall[tm] = normalize(filtered, window).astype(bf16)
+
     picked = lax.dot_general(chosen, xall[tm], TN, preferred_element_type=f32)
     for t in range(SEG):
         for h in range(2):
@@ -168,9 +169,9 @@
     )
     halves.start()
 
-    pl.semaphore_wait(beside, 3)
-    signal(beyond, in_tm(across))
-
+    signal(beside, in_tm(left))
+    signal(beside, next_along_y(tm))
+    signal(beside, next_along_y(across))
 
     halves.wait_recv()
     for t in range(SEG):
@@ -186,6 +187,8 @@
         )
         pl.when(place != k)(copy.start)
 
+    pl.semaphore_wait(beside, 3)
+    signal(beyond, in_tm(across))
     pl.semaphore_wait(beyond, 1)
     gather = [
         pltpu.make_async_remote_copy(
@@ -200,11 +203,11 @@
         for d in range(1, SEG):
             signal(semaphore, in_tm(lax.rem(tm + d, SEG)))
 
-    @pl.when(sums)
-    def _():
-        pl.when(tm == owner)(lambda: announce(ready))
+    @pl.when(sums & (tm == owner))
+    def _():
+        announce(ready)
         pl.semaphore_wait(column, SIDE - SEG)
-        pl.when(tm == owner)(lambda: announce(complete))
+        announce(complete)
 
     @pl.when(sums)
     def _():
@@ -217,21 +220,20 @@
         pl.when(tm != owner)(lambda: pl.semaphore_wait(ready, 1))
 
         def spread(p):
-            copy = pltpu.make_async_remote_copy(
+            return pltpu.make_async_remote_copy(
                 mine, parts.at[core, tm], s2_send, s2_recv.at[tm], {"tm": owner, "array": p}, MESH
             )
-            pl.when(jnp.logical_not((tm == owner) & (p == place)))(copy.start)
-
-        for p in range(0, SUMS, 2):
-            spread(p + 1)
-            spread(p)
-        pl.when(tm != owner)(lambda: pl.semaphore_wait(complete, 1))
-
-        def one_side(i, carry):
-            spread(2 * i + core)
-            return carry
-
-        lax.fori_loop(SUMS // 2, SIDE, one_side, 0)
+
+        for z_to in ORDER:
+            if z_to == ORDER[2]:
+                pl.when(tm != owner)(lambda: pl.semaphore_wait(complete, 1))
+            for side_to in range(2):
+                p = z_to * NYC + 2 * side_to
+                if p < SUMS:
+                    for q in (p + 1, p):
+                        pl.when(jnp.logical_not((tm == owner) & (place == q)))(spread(q).start)
+                else:
+                    spread(p + core).start()
         pl.when(tm == owner)(lambda: pltpu.make_async_copy(mine, parts.at[core, tm], s2_recv.at[tm]).start())
 
     step = iota((SAMPLES, CH), 0)

time: 29.7 us -> 28.9 us (0.973)
  Pallas kernels: 28.8 us -> 28 us
    pallas_call x1, Pallas kernels: 28.8 us -> 28 us  [body(): pl.pallas_call(kernel, out_shape=pltpu.VMEM((LAGS, ROWS, CH), bf16), in_s...]
where the time goes in v7:
time: 28.9 us; the launch traced here: 28.8 us
  Pallas kernels  28 us (97%)
  local copies, waits for them, and re-layouts  0.76 us (3%)
    pallas_call x1, Pallas kernels, body(): pl.pallas_call(kernel, out_shape=pltpu.VMEM((LAGS, ROWS, CH), bf16), in_s...  28 us
    unnamed x1, local copies, waits for them, and re-layouts  0.76 us

profile of v7, /device:TPU:1, one launch (start us, length us, event | category | flops | bytes accessed | tf_op | source)
XLA Modules:
  0.0 28.8 jit_solution(8066580029996004115)
XLA Ops:
  0.0 28.0 %shard_map.37 = bf16[101,16,128]{2,1,0:T(8,128)(2,1)S(1)} custom-call(bf16[1,128,1024]{2,1,0:T(8,128)(2,1)} %raw_hbm.1, f32[8]{0:T(128)} %taps_hbm.1, s32[4,32]{1,0:T(4,128)} %ids_hbm.1), custom_call_target="tpu_custom_call" | custom-call | tf_op jit(solution)/shard_map/pallas_call | solution.py:326
  28.1 0.8 %copy.5 = bf16[16,101,128]{2,0,1:T(8,128)(2,1)} copy(bf16[16,101,128]{2,0,1:T(8,128)(2,1)S(1)} %bitcast.1) | data formatting | bytes 827392

commit v8 on v7

--- a/solution.py
+++ b/solution.py
@@ -23,10 +23,10 @@
 NZ = 16
 NYC = 4
 PLACES = NZ * NYC
+FIRST = 1
 SUMS = 16
 SIDE = PLACES // 2
-ORDER = (0, 1, 4, 5, 2, 3, 6, 10, 7, 9, 8, 11, 12, 13, 14, 15)
-AWAIT = {0: 4, 4: 8}
+ORDER = (0, 1, 4, 5, 2, 6, 9, 10, 3, 7, 8, 11, 12, 13, 14, 15)
 USERS = SUMS + (PLACES - SUMS) // 2
 UP = 26
 DOWN = 25
@@ -107,6 +107,7 @@
     other = place + 1 - 2 * core
     sums = place < SUMS
     owner = 2 * z + 1 - side
+    both = sums & (side == 1) & (z < FIRST)
 
     right, left = lax.rem(tm + 2, SEG), lax.rem(tm + 6, SEG)
     across = tm + 1 - 2 * lax.rem(tm, 2)
@@ -135,8 +136,19 @@
             signal(barrier, {"tm": tm, "array": lax.rem(place + 2 * d, PLACES)})
             return carry
 
-        for k in range(0, SUMS, 2):
-            signal(barrier, {"tm": tm, "array": k + 1 - core})
+        def greet_other(d, carry):
+            signal(barrier, {"tm": tm, "array": lax.rem(other + 2 * d, PLACES)})
+            return carry
+
+        @pl.when(jnp.logical_not(both))
+        def _():
+            for k in range(0, SUMS, 2):
+                signal(barrier, {"tm": tm, "array": k + 1 - core})
+
+        @pl.when(both)
+        def _():
+            lax.fori_loop(0, SIDE, greet_other, 0)
+
         lax.fori_loop(1, SIDE, greet, 0)
 
     inputs[1].wait()
@@ -151,7 +163,7 @@
     inputs[0].wait()
     filtered = decimate(raw[0], bands)
 
-    pl.semaphore_wait(barrier, jnp.where(sums, SUMS - 1, SEG + 1) + 4)
+    pl.semaphore_wait(barrier, jnp.where(sums, SUMS - 1, SEG + FIRST + 1) + 4)
 
     mine_at = lax.div(tm, 2) * NYC + 2 * (1 - lax.rem(tm, 2)) + core
     pl.when(jnp.logical_not(sums))(lambda: signal(column, {"tm": tm, "array": mine_at}))
@@ -162,30 +174,36 @@
     for t in range(SEG):
         for h in range(2):
             part = picked[ROWS * t + 8 * h : ROWS * t + 8 * h + 8]
-            send0[h, t] = jnp.concatenate([part[:, :128], part[:, 128:]], 0).astype(bf16)
+            send0[h, t // 2 + 4 * (t % 2)] = jnp.concatenate([part[:, :128], part[:, 128:]], 0).astype(bf16)
 
     halves = pltpu.make_async_remote_copy(
-        send0.at[1 - core], recv0, s0_send, s0_recv, {"tm": tm, "array": other}, MESH
+        send0.at[1 - core, pl.ds(FIRST, SEG - FIRST)], recv0, s0_send, s0_recv, {"tm": tm, "array": other}, MESH
     )
     halves.start()
+
+    def to_sum(chunk, k):
+        slot = lax.rem(place - k + PLACES, PLACES)
+        return pltpu.make_async_remote_copy(
+            chunk, recv1.at[slot], s1_send, s1_recv, {"tm": tm, "array": k}, MESH
+        )
+
+    for plane in range(FIRST):
+        k = plane * NYC + 2 + core
+        pl.when(place != k)(to_sum(send0.at[core, plane], k).start)
+        to_sum(send0.at[1 - core, plane], plane * NYC + 3 - core).start()
 
     signal(beside, in_tm(left))
     signal(beside, next_along_y(tm))
     signal(beside, next_along_y(across))
 
     halves.wait_recv()
-    for t in range(SEG):
-        send1[t] = (send0[core, t].astype(f32) + recv0[t].astype(f32)).astype(bf16)
-
-    for i in range(SEG):
-        plane = jnp.where(z < 10, i // 2, 3 - i // 2)
-        to_side = lax.rem(side + 1 + i, 2)
-        k = plane * NYC + 2 * to_side + core
-        copy = pltpu.make_async_remote_copy(
-            send1.at[2 * plane + 1 - to_side], recv1.at[lax.div(lax.rem(place - k + PLACES, PLACES), 2)],
-            s1_send, s1_recv, {"tm": tm, "array": k}, MESH,
-        )
-        pl.when(place != k)(copy.start)
+    rest = [4, 1, 5, 2, 6, 3, 7]
+    for near, far in zip(rest, reversed(rest), strict=True):
+        chunk = jnp.where(z < 10, near, far)
+        i = chunk - FIRST
+        k = jnp.where(chunk < 4, chunk * NYC + 2, (chunk - 4) * NYC) + core
+        send1[i] = (send0[core, chunk].astype(f32) + recv0[i].astype(f32)).astype(bf16)
+        pl.when(place != k)(to_sum(send1.at[i], k).start)
 
     pl.semaphore_wait(beside, 3)
     signal(beyond, in_tm(across))
@@ -211,12 +229,25 @@
 
     @pl.when(sums)
     def _():
-        others = recv1.at[pl.ds(1, SIDE - 1)]
-        pltpu.make_async_copy(others, others, s1_recv).wait()
-        total = send1[owner].astype(f32)
-        for i in range(1, SIDE):
-            total = total + recv1[i].astype(f32)
-        mine[...] = total.astype(bf16)
+
+        @pl.when(jnp.logical_not(both))
+        def _():
+            others = recv1.at[pl.ds(0, SIDE - 1)]
+            pltpu.make_async_copy(others, others, s1_recv).wait()
+            total = send1[jnp.where(side == 1, z, z + 4) - FIRST].astype(f32)
+            for i in range(2, PLACES, 2):
+                total = total + recv1[i].astype(f32)
+            mine[...] = total.astype(bf16)
+
+        @pl.when(both)
+        def _():
+            others = recv1.at[pl.ds(0, PLACES - 1)]
+            pltpu.make_async_copy(others, others, s1_recv).wait()
+            total = send0[core, z].astype(f32)
+            for i in range(1, PLACES):
+                total = total + recv1[i].astype(f32)
+            mine[...] = total.astype(bf16)
+
         pl.when(tm != owner)(lambda: pl.semaphore_wait(ready, 1))
 
         def spread(p):
@@ -261,33 +292,45 @@
 
     lane = iota((ROWS, 128), 1)
     none = jnp.zeros((ROWS, 128), bf16)
-    rising = jnp.zeros((ROWS * UP, 2 * CH), f32)
-    falling = jnp.zeros((ROWS * DOWN, 2 * CH), f32)
-    order = [lax.rem(g, SEG) for g in (tm, right, left, across, tm + 4, across + 2, across + 6, across + 4)]
-    pair = send1.at[pl.ds(0, 2)]
-    for i, g in enumerate(order):
-        if i in AWAIT:
-
-            @pl.when(sums)
-            def _():
-                for j in range(i, AWAIT[i]):
-                    pltpu.make_async_copy(pair, pair, s2_recv.at[order[j]]).wait()
-
-        one = parts[0, g].astype(f32)
-        two = parts[1, g].astype(f32)
-        low = jnp.concatenate([one[:8], two[:8]], 0).astype(bf16)
-        high = jnp.concatenate([one[8:], two[8:]], 0).astype(bf16)
-        later, earlier = [], []
+
+    def later(low, high):
+        rows = []
         for i in range(UP):
             q = 2 * i
             lo, hi = (pltpu.roll(low, q, 1), pltpu.roll(high, q, 1)) if q else (low, high)
-            later.append(jnp.concatenate([jnp.where(lane < q, none, lo), jnp.where(lane < q, lo, hi)], 1))
+            rows.append(jnp.concatenate([jnp.where(lane < q, none, lo), jnp.where(lane < q, lo, hi)], 1))
+        return jnp.concatenate(rows, 0)
+
+    def earlier(low, high):
+        rows = []
         for i in range(DOWN):
             q = 128 - (2 * i + 1)
             lo, hi = pltpu.roll(low, q, 1), pltpu.roll(high, q, 1)
-            earlier.append(jnp.concatenate([jnp.where(lane < q, lo, hi), jnp.where(lane < q, hi, none)], 1))
-        rising = rising + jnp.dot(jnp.concatenate(later, 0), rhs_up[g], preferred_element_type=f32)
-        falling = falling + jnp.dot(jnp.concatenate(earlier, 0), rhs_down[g], preferred_element_type=f32)
+            rows.append(jnp.concatenate([jnp.where(lane < q, lo, hi), jnp.where(lane < q, hi, none)], 1))
+        return jnp.concatenate(rows, 0)
+
+    order = [lax.rem(g, SEG) for g in (tm, right, left, across, tm + 4, across + 2, across + 6, across + 4)]
+    pair = send1.at[pl.ds(0, 2)]
+    rising = jnp.zeros((ROWS * UP, 2 * CH), f32)
+    falling = jnp.zeros((ROWS * DOWN, 2 * CH), f32)
+    for group in (order[: SEG // 2], order[SEG // 2 :]):
+
+        @pl.when(sums)
+        def _():
+            for g in group:
+                pltpu.make_async_copy(pair, pair, s2_recv.at[g]).wait()
+
+        halves_of = []
+        for g in group:
+            one = parts[0, g].astype(f32)
+            two = parts[1, g].astype(f32)
+            low = jnp.concatenate([one[:8], two[:8]], 0).astype(bf16)
+            high = jnp.concatenate([one[8:], two[8:]], 0).astype(bf16)
+            halves_of.append((low, high))
+        for g, lh in zip(group, halves_of, strict=True):
+            rising = rising + jnp.dot(later(*lh), rhs_up[g], preferred_element_type=f32)
+        for g, lh in zip(group, halves_of, strict=True):
+            falling = falling + jnp.dot(earlier(*lh), rhs_down[g], preferred_element_type=f32)
 
     for i in range(UP):
         block = (rising[ROWS * i : ROWS * (i + 1)] * SCALE).astype(bf16)
@@ -308,14 +351,16 @@
 
     @pl.when(jnp.logical_not(sums))
     def _():
-        pltpu.make_async_copy(send1, send1, s1_send).wait()
+        sent = recv1.at[pl.ds(0, SEG + FIRST)]
+        pltpu.make_async_copy(sent, sent, s1_send).wait()
 
     @pl.when(sums)
     def _():
-        fewer = send1.at[pl.ds(1, SEG - 1)]
-        pltpu.make_async_copy(fewer, fewer, s1_send).wait()
-        others = recv1.at[pl.ds(1, USERS - 1)]
-        pl.when(tm != owner)(lambda: pltpu.make_async_copy(recv1, recv1, s2_send).wait())
+        sent = recv1.at[pl.ds(0, SEG + FIRST - 1)]
+        pltpu.make_async_copy(sent, sent, s1_send).wait()
+        users = recv1.at[pl.ds(0, USERS)]
+        others = recv1.at[pl.ds(0, USERS - 1)]
+        pl.when(tm != owner)(lambda: pltpu.make_async_copy(users, users, s2_send).wait())
         pl.when(tm == owner)(lambda: pltpu.make_async_copy(others, others, s2_send).wait())
 
 
@@ -334,9 +379,9 @@
             pltpu.VMEM((4, 32), jnp.int32),
             pltpu.VMEM((SEG, CH, SAMPLES), bf16),
             pltpu.VMEM((2, SEG, 16, 128), bf16),
-            pltpu.VMEM((SEG, 16, 128), bf16),
-            pltpu.VMEM((SEG, 16, 128), bf16),
-            pltpu.VMEM((USERS, 16, 128), bf16),
+            pltpu.VMEM((SEG - FIRST, 16, 128), bf16),
+            pltpu.VMEM((SEG - FIRST, 16, 128), bf16),
+            pltpu.VMEM((PLACES, 16, 128), bf16),
             pltpu.VMEM((16, 128), bf16),
             pltpu.VMEM((2, SEG, 16, 128), bf16),
             pltpu.VMEM((SEG, SAMPLES, 2 * CH), bf16),

time: 28.9 us -> 28.7 us (level)
  no operation moved by 1% of the time
where the time goes in v8:
time: 28.7 us; the launch traced here: 28.6 us
  Pallas kernels  27.9 us (97%)
  local copies, waits for them, and re-layouts  0.76 us (3%)
    pallas_call x1, Pallas kernels, body(): pl.pallas_call(kernel, out_shape=pltpu.VMEM((LAGS, ROWS, CH), bf16), in_s...  27.9 us
    unnamed x1, local copies, waits for them, and re-layouts  0.76 us

profile of v8, /device:TPU:1, one launch (start us, length us, event | category | flops | bytes accessed | tf_op | source)
XLA Modules:
  0.0 28.6 jit_solution(7672473333740666143)
XLA Ops:
  0.0 27.9 %shard_map.37 = bf16[101,16,128]{2,1,0:T(8,128)(2,1)S(1)} custom-call(bf16[1,128,1024]{2,1,0:T(8,128)(2,1)} %raw_hbm.1, f32[8]{0:T(128)} %taps_hbm.1, s32[4,32]{1,0:T(4,128)} %ids_hbm.1), custom_call_target="tpu_custom_call" | custom-call | tf_op jit(solution)/shard_map/pallas_call | solution.py:371
  27.9 0.8 %copy.5 = bf16[16,101,128]{2,0,1:T(8,128)(2,1)} copy(bf16[16,101,128]{2,0,1:T(8,128)(2,1)S(1)} %bitcast.1) | data formatting | bytes 827392

commit v9 on v8

--- a/solution.py
+++ b/solution.py
@@ -329,15 +329,16 @@
             halves_of.append((low, high))
         for g, lh in zip(group, halves_of, strict=True):
             rising = rising + jnp.dot(later(*lh), rhs_up[g], preferred_element_type=f32)
+        if group[-1] is order[-1]:
+            for i in range(UP):
+                block = (rising[ROWS * i : ROWS * (i + 1)] * SCALE).astype(bf16)
+                lag = MAXLAG + 2 * i
+                out_ref[lag] = block[:, :CH]
+                if lag + 1 < LAGS:
+                    out_ref[lag + 1] = block[:, CH:]
         for g, lh in zip(group, halves_of, strict=True):
             falling = falling + jnp.dot(earlier(*lh), rhs_down[g], preferred_element_type=f32)
 
-    for i in range(UP):
-        block = (rising[ROWS * i : ROWS * (i + 1)] * SCALE).astype(bf16)
-        lag = MAXLAG + 2 * i
-        out_ref[lag] = block[:, :CH]
-        if lag + 1 < LAGS:
-            out_ref[lag + 1] = block[:, CH:]
     for i in range(DOWN):
         block = (falling[ROWS * i : ROWS * (i + 1)] * SCALE).astype(bf16)
         lag = MAXLAG - 1 - 2 * i

time: 28.7 us -> 28.7 us (level)
  no operation moved by 1% of the time
where the time goes in v9:
time: 28.7 us; the launch traced here: 28.6 us
  Pallas kernels  27.9 us (97%)
  local copies, waits for them, and re-layouts  0.76 us (3%)
    pallas_call x1, Pallas kernels, body(): pl.pallas_call(kernel, out_shape=pltpu.VMEM((LAGS, ROWS, CH), bf16), in_s...  27.9 us
    unnamed x1, local copies, waits for them, and re-layouts  0.76 us

profile of v9, /device:TPU:1, one launch (start us, length us, event | category | flops | bytes accessed | tf_op | source)
XLA Modules:
  0.0 28.6 jit_solution(7672473333740666143)
XLA Ops:
  0.0 27.9 %shard_map.37 = bf16[101,16,128]{2,1,0:T(8,128)(2,1)S(1)} custom-call(bf16[1,128,1024]{2,1,0:T(8,128)(2,1)} %raw_hbm.1, f32[8]{0:T(128)} %taps_hbm.1, s32[4,32]{1,0:T(4,128)} %ids_hbm.1), custom_call_target="tpu_custom_call" | custom-call | tf_op jit(solution)/shard_map/pallas_call | solution.py:372
  27.9 0.8 %copy.5 = bf16[16,101,128]{2,0,1:T(8,128)(2,1)} copy(bf16[16,101,128]{2,0,1:T(8,128)(2,1)S(1)} %bitcast.1) | data formatting | bytes 827392

commit v10 on v9

--- a/solution.py
+++ b/solution.py
@@ -179,7 +179,6 @@
     halves = pltpu.make_async_remote_copy(
         send0.at[1 - core, pl.ds(FIRST, SEG - FIRST)], recv0, s0_send, s0_recv, {"tm": tm, "array": other}, MESH
     )
-    halves.start()
 
     def to_sum(chunk, k):
         slot = lax.rem(place - k + PLACES, PLACES)
@@ -191,6 +190,8 @@
         k = plane * NYC + 2 + core
         pl.when(place != k)(to_sum(send0.at[core, plane], k).start)
         to_sum(send0.at[1 - core, plane], plane * NYC + 3 - core).start()
+
+    halves.start()
 
     signal(beside, in_tm(left))
     signal(beside, next_along_y(tm))

time: 28.7 us -> 28.7 us (level)
  no operation moved by 1% of the time
where the time goes in v10:
time: 28.7 us; the launch traced here: 28.6 us
  Pallas kernels  27.9 us (97%)
  local copies, waits for them, and re-layouts  0.76 us (3%)
    pallas_call x1, Pallas kernels, body(): pl.pallas_call(kernel, out_shape=pltpu.VMEM((LAGS, ROWS, CH), bf16), in_s...  27.9 us
    unnamed x1, local copies, waits for them, and re-layouts  0.76 us

profile of v10, /device:TPU:1, one launch (start us, length us, event | category | flops | bytes accessed | tf_op | source)
XLA Modules:
  0.0 28.6 jit_solution(16890078681909379918)
XLA Ops:
  0.0 27.9 %shard_map.37 = bf16[101,16,128]{2,1,0:T(8,128)(2,1)S(1)} custom-call(bf16[1,128,1024]{2,1,0:T(8,128)(2,1)} %raw_hbm.1, f32[8]{0:T(128)} %taps_hbm.1, s32[4,32]{1,0:T(4,128)} %ids_hbm.1), custom_call_target="tpu_custom_call" | custom-call | tf_op jit(solution)/shard_map/pallas_call | solution.py:373
  27.9 0.8 %copy.5 = bf16[16,101,128]{2,0,1:T(8,128)(2,1)} copy(bf16[16,101,128]{2,0,1:T(8,128)(2,1)S(1)} %bitcast.1) | data formatting | bytes 827392

commit v11 on v9

--- a/solution.py
+++ b/solution.py
@@ -313,7 +313,7 @@
     pair = send1.at[pl.ds(0, 2)]
     rising = jnp.zeros((ROWS * UP, 2 * CH), f32)
     falling = jnp.zeros((ROWS * DOWN, 2 * CH), f32)
-    for group in (order[: SEG // 2], order[SEG // 2 :]):
+    for group in (order[:5], order[5:]):
 
         @pl.when(sums)
         def _():

time: 28.7 us -> 29.3 us (1.021)
  Pallas kernels: 27.9 us -> 28.4 us
    pallas_call x1, Pallas kernels: 27.9 us -> 28.4 us  [body(): pl.pallas_call(kernel, out_shape=pltpu.VMEM((LAGS, ROWS, CH), bf16), in_s...]
where the time goes in v11:
time: 29.3 us; the launch traced here: 29.1 us
  Pallas kernels  28.4 us (97%)
  local copies, waits for them, and re-layouts  0.76 us (3%)
    pallas_call x1, Pallas kernels, body(): pl.pallas_call(kernel, out_shape=pltpu.VMEM((LAGS, ROWS, CH), bf16), in_s...  28.4 us
    unnamed x1, local copies, waits for them, and re-layouts  0.76 us

profile of v11, /device:TPU:1, one launch (start us, length us, event | category | flops | bytes accessed | tf_op | source)
XLA Modules:
  0.0 29.1 jit_solution(6991518190839559195)
XLA Ops:
  0.0 28.4 %shard_map.37 = bf16[101,16,128]{2,1,0:T(8,128)(2,1)S(1)} custom-call(bf16[1,128,1024]{2,1,0:T(8,128)(2,1)} %raw_hbm.1, f32[8]{0:T(128)} %taps_hbm.1, s32[4,32]{1,0:T(4,128)} %ids_hbm.1), custom_call_target="tpu_custom_call" | custom-call | tf_op jit(solution)/shard_map/pallas_call | solution.py:372
  28.4 0.8 %copy.5 = bf16[16,101,128]{2,0,1:T(8,128)(2,1)} copy(bf16[16,101,128]{2,0,1:T(8,128)(2,1)S(1)} %bitcast.1) | data formatting | bytes 827392
